TPU v7x, 128 devices: a whole 4x4x4 slice. The times are simulated.
128 devices in a mesh: seq: 32 (over z, y_lo, x), tp: 4 (over y_hi, core).
Axes of the slice: x: 4, y: 4 (y_hi: 2, y_lo: 2; y = y_hi * 2 + y_lo), z: 4, core: 2. Of those that a mesh axis runs over, the one named last changes fastest.
Arguments:
- hidden: bfloat16 [8192, 3072], P('seq'), may hold values from -6 to 6
- qkv_weight: bfloat16 [3072, 3, 1536], P(None, None, 'tp'), may hold values from -0.109375 to 0.109375
- cotangent: bfloat16 [8192, 1536], P('seq', 'tp'), may hold values from -6 to 6
Outputs:
- attention: bfloat16 [8192, 1536], P('seq', 'tp')
- grad_hidden: bfloat16 [8192, 3072], P('seq', 'tp')
- grad_weight: float32 [3072, 3, 1536], P('seq', None, 'tp')
All inputs are finite; a program needn't handle non-finite values.
Results may differ from a plain program's by a relative error of at most 0.023.
Values may be sent and summed in bfloat16 or wider, within the bound.
A program may use at most 128 MiB of HBM per device.

v0:
```python
import math

import jax
import jax.numpy as jnp
from jax import lax
from jax.sharding import PartitionSpec as P

HD = 128


def on_device(hidden, qkv_weight, cotangent):
    softmax_scale = 1.0 / math.sqrt(HD)
    tok_rows = hidden.shape[0]
    heads_local = qkv_weight.shape[2] // HD
    projected = jnp.einsum(
        "td,dcj->tcj", hidden, qkv_weight, preferred_element_type=jnp.float32
    ).astype(jnp.bfloat16)
    query_rows = projected[:, 0].reshape(tok_rows, heads_local, HD)
    key_rows = projected[:, 1].reshape(tok_rows, heads_local, HD)
    value_rows = projected[:, 2].reshape(tok_rows, heads_local, HD)
    keys_all, values_all = (
        lax.all_gather(key_rows, "seq", axis=0, tiled=True),
        lax.all_gather(value_rows, "seq", axis=0, tiled=True),
    )
    scores = (
        jnp.einsum("qhd,khd->hqk", query_rows, keys_all, preferred_element_type=jnp.float32)
        * softmax_scale
    )
    top_score = jnp.max(scores, axis=-1, keepdims=True)
    log_total = top_score + jnp.log(jnp.sum(jnp.exp(scores - top_score), axis=-1, keepdims=True))
    weights = jnp.exp(scores - log_total).astype(jnp.bfloat16)
    output_heads = jnp.einsum(
        "hqk,khd->qhd", weights, values_all, preferred_element_type=jnp.float32
    ).astype(jnp.bfloat16)
    attention = output_heads.reshape(tok_rows, heads_local * HD)
    grad_out = cotangent.reshape(tok_rows, heads_local, HD)
    row_delta = jnp.sum(grad_out.astype(jnp.float32) * output_heads.astype(jnp.float32), axis=-1)
    grad_probs = jnp.einsum(
        "qhd,khd->hqk", grad_out, values_all, preferred_element_type=jnp.float32
    )
    grad_scores = (weights.astype(jnp.float32) * (grad_probs - row_delta.T[:, :, None])).astype(
        jnp.bfloat16
    )
    grad_query = (
        jnp.einsum("hqk,khd->qhd", grad_scores, keys_all, preferred_element_type=jnp.float32)
        * softmax_scale
    ).astype(jnp.bfloat16)
    log_rows = log_total[:, :, 0].T
    queries_all, grads_all = (
        lax.all_gather(query_rows, "seq", axis=0, tiled=True),
        lax.all_gather(grad_out, "seq", axis=0, tiled=True),
    )
    log_all, delta_all = (
        lax.all_gather(log_rows, "seq", axis=0, tiled=True),
        lax.all_gather(row_delta, "seq", axis=0, tiled=True),
    )
    key_scores = (
        jnp.einsum("khd,qhd->hkq", key_rows, queries_all, preferred_element_type=jnp.float32)
        * softmax_scale
    )
    key_probs = jnp.exp(key_scores - log_all.T[:, None, :]).astype(jnp.bfloat16)
    key_grad_probs = jnp.einsum(
        "khd,qhd->hkq", value_rows, grads_all, preferred_element_type=jnp.float32
    )
    key_grad_scores = (
        key_probs.astype(jnp.float32) * (key_grad_probs - delta_all.T[:, None, :])
    ).astype(jnp.bfloat16)
    grad_key = (
        jnp.einsum("hkq,qhd->khd", key_grad_scores, queries_all, preferred_element_type=jnp.float32)
        * softmax_scale
    ).astype(jnp.bfloat16)
    grad_value = jnp.einsum(
        "hkq,qhd->khd", key_probs, grads_all, preferred_element_type=jnp.float32
    ).astype(jnp.bfloat16)
    grad_proj = jnp.stack([grad_query, grad_key, grad_value], axis=1).reshape(
        tok_rows, 3, heads_local * HD
    )
    hidden_terms = jnp.einsum(
        "tcj,dcj->td", grad_proj, qkv_weight, preferred_element_type=jnp.float32
    )
    grad_hidden = lax.psum_scatter(hidden_terms, "tp", scatter_dimension=1, tiled=True).astype(
        jnp.bfloat16
    )
    grad_weight = lax.psum_scatter(
        jnp.einsum("tr,tcj->rcj", hidden, grad_proj, preferred_element_type=jnp.float32),
        "seq",
        scatter_dimension=0,
        tiled=True,
    )
    return (attention, grad_hidden, grad_weight)


def solution(mesh):
    in_specs = (P("seq", None), P(None, None, "tp"), P("seq", "tp"))
    out_specs = (P("seq", "tp"), P("seq", "tp"), P("seq", None, "tp"))
    return jax.shard_map(
        on_device, mesh=mesh, in_specs=in_specs, out_specs=out_specs, check_vma=False
    )
```

profile of v0, /device:TPU:16, one launch (start us, length us, event | category | flops | bytes accessed | tf_op | source)
XLA Modules:
  0.0 936.7 jit_solution(12319128629582567495)
XLA Ops:
  7.2 0.0 copy-start
  7.2 0.0 copy-start.3
  7.2 0.0 all-gather.7.cloned.1.call-start
  7.2 1.3 copy-done
  8.6 5.2 fusion.8
  13.8 0.1 fusion.20
  13.9 0.1 copy.38
  14.0 0.8 copy.39
  14.8 0.0 all-gather.7.cloned.1.call-update
  14.8 0.0 all-gather.5.cloned.1.call-start
  14.9 0.8 copy.36
  15.7 0.0 all-gather.5.cloned.1.call-update
  15.7 0.0 all-gather.9.cloned.1.call-start
  15.8 0.1 copy.37
  15.9 0.8 copy.46
  16.8 0.0 all-gather.9.cloned.1.call-update
  16.8 0.0 all-gather.11.cloned.1.call-start
  16.8 0.0 copy-done.3
  16.8 0.8 copy.41
  17.7 0.0 all-gather.11.cloned.1.call-update
  17.7 0.0 reduce-scatter.5.cloned.1.call-start
  17.7 162.1 %all-gather.7.cloned.1.call-done = bf16[8192,3,128]{2,0,1:T(8,128)(2,1)} async-done(((bf16[256,3,128]{2,0,1:T(8,128)(2,1)}), bf16[8192,3,128]{2,0,1:T(8,128)(2,1)}) %all-gather.7.cloned.1.call-update) | async-done | bytes 6291472 | tf_op jit(solution)/shard_map/all_gather | solution.py:22
  179.8 13.0 %multiply_reduce_fusion = (f32[3,256]{1,0:T(4,128)S(1)}, f32[3,256,8192]{2,1,0:T(8,128)}) fusion(bf16[256,3,128]{0,2,1:T(8,128)(2,1)S(1)} %bitcast.66, bf16[8192,3,128]{2,0,1:T(8,128)(2,1)} %all-gather.7.cloned.1.call-done), kind=kOutput, calls=%fused_computation.6 | convolution fusion | flops 1623194880 | bytes 31656960 | tf_op jit(solution)/shard_map/qhd,khd->hqk/dot_general | solution.py:26
  192.9 0.0 copy-start.1
  192.9 10.9 %exponential_reduce_fusion = f32[3,256]{1,0:T(4,128)S(1)} fusion(f32[3,256,8192]{2,1,0:T(8,128)} %get-tuple-element.16, f32[3,256]{1,0:T(4,128)S(1)} %get-tuple-element.15), kind=kLoop, calls=%fused_computation.5 | loop fusion | flops 18873600 | bytes 25171968 | tf_op jit(solution)/shard_map/reduce_sum | solution.py:30
  203.8 130.3 %all-gather.5.cloned.1.call-done = bf16[8192,3,128]{0,2,1:T(8,128)(2,1)} async-done(((bf16[256,3,128]{0,2,1:T(8,128)(2,1)}), bf16[8192,3,128]{0,2,1:T(8,128)(2,1)}) %all-gather.5.cloned.1.call-update) | async-done | bytes 6291472 | tf_op jit(solution)/shard_map/all_gather | solution.py:23
  334.1 0.0 copy-done.1
  334.1 12.7 %multiply_reduce_fusion.1 = (f32[256,3]{0,1:T(4,128)S(1)}, bf16[3,128,256]{2,1,0:T(8,128)(2,1)S(1)}) fusion(bf16[256,3,128]{0,2,1:T(8,128)(2,1)S(1)} %bitcast.63, bf16[8192,3,128]{0,2,1:T(8,128)(2,1)} %all-gather.5.cloned.1.call-done, f32[3,256,8192]{2,1,0:T(8,128)} %get-tuple-element.16, f32[3,256]{1,0:T(4,128)S(1)} %log_add_fusion), kind=kOutput, calls=%fused_computation.23 | convolution fusion | flops 1629977856 | bytes 31856640 | tf_op jit(solution)/shard_map/hqk,khd->qhd/dot_general | solution.py:32
  346.8 14.9 %fusion.13 = bf16[3,128,256]{2,1,0:T(8,128)(2,1)S(1)} fusion(bf16[8192,3,128]{2,0,1:T(8,128)(2,1)} %all-gather.7.cloned.1.call-done, bf16[8192,3,128]{0,2,1:T(8,128)(2,1)} %all-gather.5.cloned.1.call-done, bf16[256,3,128]{0,2,1:T(8,128)(2,1)S(1)} %bitcast.64, f32[3,256]{1,0:T(4,128)S(1)} %bitcast.78, f32[3,256]{1,0:T(4,128)S(1)} %log_add_fusion, ...), kind=kOutput, calls=%fused_computation.19 | convolution fusion | flops 3265462272 | bytes 38148096 | tf_op jit(solution)/shard_map/hqk,khd->qhd/dot_general | solution.py:45
  361.7 0.0 copy-start.2
  361.7 0.2 copy.51
  361.9 81.4 %all_gather.23 = f32[8192,3]{0,1:T(4,128)S(1)} all-gather(f32[256,3]{0,1:T(4,128)S(1)} %get-tuple-element.17), channel_id=1, replica_groups=mesh['seq'=32,'tp'=4] {'seq'}, dimensions={0}, use_global_device_ids=true | all-gather | bytes 101376 | tf_op jit(solution)/shard_map/all_gather | solution.py:55
  443.3 76.1 %all_gather.21 = f32[8192,3]{0,1:T(4,128)S(1)} all-gather(f32[256,3]{0,1:T(4,128)S(1)} %bitcast.77), channel_id=1, replica_groups=mesh['seq'=32,'tp'=4] {'seq'}, dimensions={0}, use_global_device_ids=true | all-gather | bytes 101376 | tf_op jit(solution)/shard_map/all_gather | solution.py:54
  519.4 0.0 all-gather.9.cloned.1.call-done
  519.4 10.6 %exponential_convert_fusion = bf16[3,256,8192]{2,1,0:T(8,128)(2,1)} fusion(bf16[256,3,128]{0,2,1:T(8,128)(2,1)S(1)} %bitcast.70, bf16[8192,3,128]{2,0,1:T(8,128)(2,1)} %all-gather.9.cloned.1.call-done, f32[3,8192]{1,0:T(4,128)S(1)} %bitcast.76), kind=kOutput, calls=%fused_computation.3 | convolution fusion | flops 1629487104 | bytes 19169280 | tf_op jit(solution)/shard_map/khd,qhd->hkq/dot_general | solution.py:58
  529.9 124.4 %all-gather.11.cloned.1.call-done = bf16[8192,3,128]{0,2,1:T(8,128)(2,1)} async-done(((bf16[256,3,128]{0,2,1:T(8,128)(2,1)}), bf16[8192,3,128]{0,2,1:T(8,128)(2,1)}) %all-gather.11.cloned.1.call-update) | async-done | bytes 6291472 | tf_op jit(solution)/shard_map/all_gather | solution.py:51
  654.3 0.0 copy-done.2
  654.3 12.5 %fusion.15 = bf16[3,128,256]{2,1,0:T(8,128)(2,1)S(1)} fusion(bf16[8192,3,128]{2,0,1:T(8,128)(2,1)} %all-gather.9.cloned.1.call-done, bf16[3,256,8192]{2,1,0:T(8,128)(2,1)} %exponential_convert_fusion, bf16[256,3,128]{0,2,1:T(8,128)(2,1)S(1)} %bitcast.72, bf16[8192,3,128]{0,2,1:T(8,128)(2,1)} %all-gather.11.cloned.1.call-done, f32[3,8192]{1,0:T(4,128)S(1)} %bitcast.75), kind=kOutput, calls=%fused_computation.21 | convolution fusion | flops 3246587904 | bytes 25657344 | tf_op jit(solution)/shard_map/hkq,qhd->khd/dot_general | solution.py:69
  666.8 0.2 copy.52
  667.0 10.7 %convolution_convert_fusion = bf16[3,256,128]{1,2,0:T(8,128)(2,1)S(1)} fusion(bf16[3,256,8192]{2,1,0:T(8,128)(2,1)} %exponential_convert_fusion, bf16[8192,3,128]{0,2,1:T(8,128)(2,1)} %all-gather.11.cloned.1.call-done), kind=kOutput, calls=%fused_computation.16 | convolution fusion | flops 1610711040 | bytes 19070976 | tf_op jit(solution)/shard_map/hkq,qhd->khd/dot_general | solution.py:72
  677.8 0.2 copy.53
  677.9 7.0 convolution_bitcast_fusion
  684.9 0.0 reduce-scatter.5.cloned.1.call-update
  684.9 0.3 reduce-scatter.7.cloned.1.call-start
  685.2 7.2 fusion.4
  692.4 15.3 %copy.69 = f32[3072,1152]{1,0:T(8,128)} copy(f32[3072,1152]{0,1:T(8,128)} %bitcast.60) | data formatting | bytes 28311552
  707.7 0.0 reduce-scatter.7.cloned.1.call-update
  707.7 0.8 copy.55
  708.6 20.5 %reduce-scatter.5.cloned.1.call-done = f32[256,768]{1,0:T(8,128)} async-done(((f32[256,3072]{1,0:T(8,128)}), f32[256,768]{1,0:T(8,128)}) %reduce-scatter.5.cloned.1.call-update) | async-done | bytes 786448 | tf_op jit(solution)/shard_map/reduce_scatter | solution.py:81
  729.0 1.9 convert_element_type.71
  730.9 196.7 %reduce-scatter.7.cloned.1.call-done = f32[96,1152]{1,0:T(8,128)} async-done(((f32[3072,1152]{1,0:T(8,128)}), f32[96,1152]{1,0:T(8,128)}) %reduce-scatter.7.cloned.1.call-update) | async-done | bytes 442384
  927.6 1.2 copy.70
  928.8 1.0 copy.56
  (1 shorter events, 0.0 us)
Async XLA Ops:
  7.2 1.4 copy-start
  7.2 9.7 %copy-start.3 = (bf16[256,384]{1,0:T(8,128)(2,1)S(1)}, bf16[256,384]{1,0:T(8,128)(2,1)}, u32[]{:S(2)}) copy-start(bf16[256,384]{1,0:T(8,128)(2,1)} %param.5) | copy-start | bytes 589828
  7.2 172.7 %all-gather.7.cloned.1.call-start = ((), (), s32[]{:S(2)}) async-start(), calls=%async_computation.3 | async-start | bytes 6488064 | tf_op jit(solution)/shard_map/all_gather | solution.py:22
  14.8 319.3 %all-gather.5.cloned.1.call-start = ((), (), s32[]{:S(2)}) async-start(), calls=%async_computation.2 | async-start | bytes 6488064 | tf_op jit(solution)/shard_map/all_gather | solution.py:23
  15.7 503.6 %all-gather.9.cloned.1.call-start = ((), (), s32[]{:S(2)}) async-start(), calls=%async_computation.4 | async-start | bytes 6488064 | tf_op jit(solution)/shard_map/all_gather | solution.py:50
  16.8 637.5 %all-gather.11.cloned.1.call-start = ((), (), s32[]{:S(2)}) async-start(), calls=%async_computation.5 | async-start | bytes 6488064 | tf_op jit(solution)/shard_map/all_gather | solution.py:51
  17.7 711.3 %reduce-scatter.5.cloned.1.call-start = ((), (), s32[]{:S(2)}) async-start(), calls=%async_computation.6 | async-start | bytes 3932160 | tf_op jit(solution)/shard_map/reduce_scatter | solution.py:81
  192.9 141.3 %copy-start.1 = (bf16[256,384]{0,1:T(8,128)(2,1)S(1)}, bf16[256,384]{0,1:T(8,128)(2,1)}, u32[]{:S(2)}) copy-start(bf16[256,384]{0,1:T(8,128)(2,1)} %copy.41) | copy-start | bytes 589828
  361.7 292.6 %copy-start.2 = (bf16[256,1,384]{0,2,1:T(8,128)(2,1)S(1)}, bf16[256,1,384]{0,2,1:T(8,128)(2,1)}, u32[]{:S(2)}) copy-start(bf16[256,1,384]{0,2,1:T(8,128)(2,1)} %copy.36) | copy-start | bytes 589828
  684.9 242.7 %reduce-scatter.7.cloned.1.call-start = ((), (), s32[]{:S(2)}) async-start(), calls=%async_computation.7 | async-start | bytes 14598144
Sparse Core Ops, SparseCore 0:
  15.0 164.8 all-gather.6
  182.0 152.0 all-gather.4
  335.8 164.7 all-gather.8
  502.5 151.7 all-gather.10
  685.1 43.9 reduce-scatter.4
  731.4 196.1 reduce-scatter.6
where the time goes:
time: 937 us
  waiting for transfers between devices  634 us (68%)
  blocking collectives  157 us (17%)
  matrix products  93.8 us (10%)
  local copies, waits for them, and re-layouts  23.9 us (3%)
  between operations  14.2 us (2%)
  other arithmetic  12.8 us (1%)
    unnamed x7, waiting for transfers between devices  197 us
    all_gather x1, waiting for transfers between devices, on_device(): lax.all_gather(key_rows, 'seq', axis=0, tiled=True)  162 us
    all_gather x1, waiting for transfers between devices, on_device(): lax.all_gather(value_rows, 'seq', axis=0, tiled=True)  130 us
    all_gather x1, waiting for transfers between devices, on_device(): lax.all_gather(grad_out, 'seq', axis=0, tiled=True)  124 us
    all_gather x1, blocking collectives, on_device(): lax.all_gather(row_delta, 'seq', axis=0, tiled=True)  81.4 us
    all_gather x1, blocking collectives, on_device(): lax.all_gather(log_rows, 'seq', axis=0, tiled=True)  76.1 us
    unnamed x13, local copies, waits for them, and re-layouts  20.6 us
    reduce_scatter x1, waiting for transfers between devices, on_device(): lax.psum_scatter(hidden_terms, 'tp', scatter_dimension=1, tiled=True)  20.5 us
  transfers between devices with their start and end apart: 6, of which 5 were waited for; matrix products, arithmetic and copies ran while one was open for 10% of the time, Pallas kernels for 0%

commit v1 on v0

v1 whole, which is shorter than its diff:
```python
import functools
import math

import jax
import jax.numpy as jnp
from jax import lax
from jax.experimental import pallas as pl
from jax.experimental.pallas import tpu as pltpu
from jax.sharding import PartitionSpec as P

HD = 128
T = 256
NZ, NY, NX = 4, 2, 4
KEYS = NZ * NY * T
CHUNK = 512
SCALE = 1.0 / math.sqrt(HD)
LOG2 = SCALE * math.log2(math.e)
MESH = pl.DeviceIdType.MESH
F32, BF16 = jnp.float32, jnp.bfloat16
NN = (((1,), (0,)), ((), ()))
NT = (((1,), (1,)), ((), ()))


def dot(a, b, dims=NN):
    return lax.dot_general(a, b, dims, preferred_element_type=F32)


def coords():
    s = lax.axis_index("seq")
    return s // (NY * NX), (s // NX) % NY, s % NX, lax.axis_index("tp")


def seq_of(z, y, x):
    return (z * NY + y) * NX + x


def aligned(i, n):
    return pl.ds(pl.multiple_of(i * n, n), n)


def attention_kernel(
    p_ref, cot_ref, ht_ref, att_ref, g_ref, hx_ref,
    own_qg, own_kv, qg, kv, vkt, pt, ut, s_buf, st, sm, sm_all, ma, cs, es, rhs, ob, ro, kb, rk,
    sem_s, sem_r, sem_os, sem_or, sem_ks, sem_kr, sem_l,
):
    z, y, x, t = coords()
    other = 1 - y
    head_a, head_b = 2 * y, 2 - 2 * y

    def at(zz, yy, xx):
        return (seq_of(zz, yy, xx), t)

    def xs(d):
        return (x + d) % NX

    def zs(d):
        return (z + d) % NZ

    for h in range(3):
        cols = slice(h * HD, (h + 1) * HD)
        own_qg[h, 0] = p_ref[0, :, cols]
        own_qg[h, 1] = cot_ref[:, cols]
        own_kv[h, 0] = p_ref[1, :, cols]
        own_kv[h, 1] = p_ref[2, :, cols]

    barrier = pltpu.get_barrier_semaphore()
    peers = [at(z, y, xs(d)) for d in (1, 2, 3)] + [at(z, other, xs(d)) for d in range(4)]
    peers += [at(zs(d), y, x) for d in (1, 2, 3)] + [at(zs(d), other, x) for d in (1, 2, 3)]
    for peer in peers:
        pl.semaphore_signal(barrier, inc=1, device_id=peer, device_id_type=MESH)
    pl.semaphore_wait(barrier, len(peers))

    def remote(i, src, dst, peer):
        return pltpu.make_async_remote_copy(
            src_ref=src, dst_ref=dst, send_sem=sem_s.at[i], recv_sem=sem_r.at[i],
            device_id=peer, device_id_type=MESH,
        )

    def qg_slot(yy, xx):
        return qg.at[4 + yy * NX + xx]

    def kv_rows(j, yy, zz):
        return kv.at[j, :, aligned(yy * NZ + zz, T), :]

    first = [
        remote(0, own_qg.at[head_b], qg_slot(y, x), at(z, other, x)),
        remote(1, own_kv.at[1], kv_rows(0, y, z), at(z, other, x)),
        remote(2, own_kv.at[head_b], kv_rows(1, y, z), at(z, other, x)),
    ]
    for d in (1, 2, 3):
        first.append(remote(2 + d, own_qg.at[1], qg.at[x], at(z, y, xs(d))))
        first.append(remote(8 + d, own_kv.at[1], kv_rows(0, y, z), at(zs(d), y, x)))
    for d in (1, 2, 3):
        first.append(remote(5 + d, own_qg.at[head_a], qg_slot(y, x), at(z, y, xs(d))))
        first.append(remote(11 + d, own_kv.at[head_a], kv_rows(1, y, z), at(zs(d), y, x)))
    for c in first:
        c.start()
    qg[x] = own_qg[1]
    qg[4 + y * NX + x] = own_qg[head_a]
    kv[0, :, aligned(y * NZ + z, T), :] = own_kv[1]
    kv[1, :, aligned(y * NZ + z, T), :] = own_kv[head_a]
    sm[...] = jnp.zeros_like(sm)
    ma[...] = jnp.zeros_like(ma)

    def got(i, dst):
        remote(i, dst, dst, at(z, other, x)).wait_recv()

    relay = []
    got(0, qg_slot(other, x))
    for d in (1, 2, 3):
        relay.append(remote(14 + d, qg_slot(other, x), qg_slot(other, x), at(z, y, xs(d))))
        relay[-1].start()
    for j in (0, 1):
        got(1 + j, kv_rows(j, other, z))
        for d in (1, 2, 3):
            rows = kv_rows(j, other, z)
            relay.append(remote(17 + 3 * j + d, rows, rows, at(zs(d), y, x)))
            relay[-1].start()
    hx_copies = [remote(26 + d, ht_ref.at[:, xs(d)], hx_ref.at[x], at(z, y, xs(d))) for d in (1, 2, 3)]
    for c in hx_copies:
        c.start()
    hx_own = pltpu.make_async_copy(ht_ref.at[:, x], hx_ref.at[x], sem_l.at[0])
    hx_own.start()

    for d in (1, 2, 3):
        got(2 + d, qg.at[xs(4 - d)])
        got(5 + d, qg_slot(y, xs(4 - d)))
        got(8 + d, kv_rows(0, y, zs(4 - d)))
        got(11 + d, kv_rows(1, y, zs(4 - d)))
        got(14 + d, qg_slot(other, xs(4 - d)))
        got(17 + d, kv_rows(0, other, zs(4 - d)))
        got(20 + d, kv_rows(1, other, zs(4 - d)))

    def transpose_block(i, _):
        for j in (0, 1):
            vkt[j, 0:HD, aligned(i, T)] = kv[j, 1, aligned(i, T), :].T
            vkt[j, HD : 2 * HD, aligned(i, T)] = kv[j, 0, aligned(i, T), :].T
        return 0

    lax.fori_loop(0, KEYS // T, transpose_block, 0)

    def unit(j, u):
        q, g = qg[u, 0], qg[u, 1]
        chunks = [slice(c * CHUNK, (c + 1) * CHUNK) for c in range(KEYS // CHUNK)]
        top = None
        for c in chunks:
            s = dot(kv[j, 0, c, :], q, NT)
            s_buf[c] = s
            m = jnp.max(s, axis=0, keepdims=True)
            top = m if top is None else jnp.maximum(top, m)
        top = top * LOG2
        total, out = 0.0, 0.0
        for c in chunks:
            p = jnp.exp2(s_buf[c] * LOG2 - top)
            total = total + jnp.sum(p, axis=0, keepdims=True)
            p = p.astype(BF16)
            pt[u, c, :] = p
            out = out + dot(vkt[j, :, c], p)
        g_t = g.astype(F32).T
        delta = jnp.sum(g_t * out[:HD], axis=0, keepdims=True) / total
        grad = 0.0
        for c in chunks:
            dp = dot(kv[j, 1, c, :], g, NT)
            d = (pt[u, c, :].astype(F32) * (dp - delta)).astype(BF16)
            ut[u, c, :] = d
            grad = grad + dot(vkt[j, HD:, c], d)
        st[u, : 2 * HD] = out
        st[u, 2 * HD :] = grad
        sm[0, pl.ds(u, 1), :] = top + jnp.log2(total)
        sm[1, pl.ds(u, 1), :] = delta
        ma[pl.ds(u, 1), :] = top
        return 0

    lax.fori_loop(0, 4, lambda u, _: unit(0, u), 0)
    lax.fori_loop(4, 12, lambda u, _: unit(1, u), 0)

    stats = [remote(23 + d, sm, sm_all.at[x], at(z, y, xs(d))) for d in (1, 2, 3)]
    for c in stats:
        c.start()
    sm_all[x] = sm[...]
    for d in (1, 2, 3):
        got(23 + d, sm_all.at[xs(4 - d)])
    lse = sm_all[:, 0]
    top = jnp.max(lse, axis=0)
    lse_all = top + jnp.log2(jnp.sum(jnp.exp2(lse - top), axis=0))
    delta = jnp.sum(jnp.exp2(lse - lse_all) * sm_all[:, 1], axis=0)
    cs[...] = jnp.exp2(ma[...] - lse_all)
    es[...] = delta - sm[1]

    def prepare(u):
        c, e = cs[pl.ds(u, 1), :], es[pl.ds(u, 1), :]
        o = st[u, 0:HD] * c
        dq = (st[u, 2 * HD :] - e * st[u, HD : 2 * HD]) * (c * SCALE)
        ob[u, 0] = o.T.astype(BF16)
        ob[u, 1] = dq.T.astype(BF16)
        cols = jnp.concatenate([c, e, jnp.zeros((6, T), F32)], axis=0).T
        c, e = cols[:, 0:1], cols[:, 1:2]
        cq = c * qg[u, 0].astype(F32)
        rhs[u, :, 0:HD] = (c * qg[u, 1].astype(F32)).astype(BF16)
        rhs[u, :, HD : 2 * HD] = (e * cq).astype(BF16)
        rhs[u, :, 2 * HD :] = cq.astype(BF16)

    def send_o(kind, d):
        xx = xs(d)
        u, h, yy = ((xx, 1, y), (4 + y * NX + xx, head_a, y), (4 + other * NX + xx, head_a, other))[kind]
        return u, pltpu.make_async_remote_copy(
            src_ref=ob.at[u], dst_ref=ro.at[h, x], send_sem=sem_os.at[kind, d], recv_sem=sem_or.at[kind, d],
            device_id=at(z, yy, xx), device_id_type=MESH,
        )

    def each_o(do):
        lax.fori_loop(1, 4, lambda d, _: do(0, d), 0)
        lax.fori_loop(0, 4, lambda d, _: do(2, d), 0)
        lax.fori_loop(1, 4, lambda d, _: do(1, d), 0)

    def prepare_send(kind, d):
        u, copy = send_o(kind, d)
        prepare(u)
        copy.start()
        return 0

    each_o(prepare_send)
    prepare(x)
    ro[1, x] = ob[x]
    prepare(4 + y * NX + x)
    ro[head_a, x] = ob[4 + y * NX + x]

    def send_k(j, own, d):
        yy = y if own else other
        zz = zs(d)
        b = j * 8 + yy * NZ + zz
        kind = 2 * j + (0 if own else 1)
        return yy * NZ + zz, b, pltpu.make_async_remote_copy(
            src_ref=kb.at[b], dst_ref=rk.at[j * 8 + y * NZ + z], send_sem=sem_ks.at[kind, d],
            recv_sem=sem_kr.at[kind, d], device_id=at(zz, yy, x), device_id_type=MESH,
        )

    def key_block(j, i, b):
        units = range(4) if j == 0 else range(4, 12)
        rows = aligned(i, T)
        dv = dk = 0.0
        for u in units:
            dv = dv + dot(pt[u, rows, :], rhs[u, :, : 2 * HD])
            dk = dk + dot(ut[u, rows, :], rhs[u, :, 2 * HD :])
        kb[b, 0] = ((dk - dv[:, HD:]) * SCALE).astype(BF16)
        kb[b, 1] = dv[:, :HD].astype(BF16)

    def key_send(j, own, d):
        i, b, copy = send_k(j, own, d)
        key_block(j, i, b)
        copy.start()
        return 0

    def each_k(do):
        for j in (0, 1):
            lax.fori_loop(0, 4, lambda d, _: do(j, False, d), 0)
            lax.fori_loop(1, 4, lambda d, _: do(j, True, d), 0)

    each_k(key_send)
    mine = y * NZ + z
    for j in (0, 1):
        key_block(j, mine, j * 8 + mine)
        rk[j * 8 + mine] = kb[j * 8 + mine]

    def finish_o(kind, d):
        _, copy = send_o(kind, d)
        copy.wait_send()
        xx = xs(4 - d)
        h = (1, head_a, head_b)[kind]
        pltpu.make_async_remote_copy(
            src_ref=ob.at[0], dst_ref=ro.at[h, xx], send_sem=sem_os.at[kind, d], recv_sem=sem_or.at[kind, d],
            device_id=at(z, other, x), device_id_type=MESH,
        ).wait_recv()
        return 0

    each_o(finish_o)
    for h in range(3):
        cols = slice(h * HD, (h + 1) * HD)
        for part in (0, 1):
            v = ro[h, 0, part].astype(F32)
            for xx in range(1, NX):
                v = v + ro[h, xx, part].astype(F32)
            if part == 0:
                att_ref[:, cols] = v.astype(BF16)
            else:
                g_ref[0, :, cols] = v.astype(BF16)

    def finish_k(j, own, d):
        _, _, copy = send_k(j, own, d)
        copy.wait_send()
        yy = y if own else other
        kind = 2 * j + (0 if own else 1)
        pltpu.make_async_remote_copy(
            src_ref=kb.at[0], dst_ref=rk.at[j * 8 + yy * NZ + zs(4 - d)], send_sem=sem_ks.at[kind, d],
            recv_sem=sem_kr.at[kind, d], device_id=at(z, other, x), device_id_type=MESH,
        ).wait_recv()
        return 0

    each_k(finish_k)
    for h, slots in ((1, range(8)), (0, range(8, 12)), (2, range(12, 16))):
        cols = slice(h * HD, (h + 1) * HD)
        for part in (0, 1):
            v = 0.0
            for i in slots:
                v = v + rk[i, part].astype(F32)
            g_ref[1 + part, :, cols] = v.astype(BF16)

    for c in first + relay + stats + hx_copies:
        c.wait_send()
    hx_own.wait()
    for d in (1, 2, 3):
        got(26 + d, hx_ref.at[xs(4 - d)])


def attention_call(projected, cotangent, hidden_t):
    scratch = [
        pltpu.VMEM((3, 2, T, HD), BF16),
        pltpu.VMEM((3, 2, T, HD), BF16),
        pltpu.VMEM((12, 2, T, HD), BF16),
        pltpu.VMEM((2, 2, KEYS, HD), BF16),
        pltpu.VMEM((2, 2 * HD, KEYS), BF16),
        pltpu.VMEM((12, KEYS, T), BF16),
        pltpu.VMEM((12, KEYS, T), BF16),
        pltpu.VMEM((KEYS, T), F32),
        pltpu.VMEM((12, 3 * HD, T), F32),
        pltpu.VMEM((2, 16, T), F32),
        pltpu.VMEM((NX, 2, 16, T), F32),
        pltpu.VMEM((16, T), F32),
        pltpu.VMEM((16, T), F32),
        pltpu.VMEM((16, T), F32),
        pltpu.VMEM((12, T, 3 * HD), BF16),
        pltpu.VMEM((12, 2, T, HD), BF16),
        pltpu.VMEM((3, NX, 2, T, HD), BF16),
        pltpu.VMEM((16, 2, T, HD), BF16),
        pltpu.VMEM((16, 2, T, HD), BF16),
        pltpu.SemaphoreType.DMA((30,)),
        pltpu.SemaphoreType.DMA((30,)),
        pltpu.SemaphoreType.DMA((3, 4)),
        pltpu.SemaphoreType.DMA((3, 4)),
        pltpu.SemaphoreType.DMA((4, 4)),
        pltpu.SemaphoreType.DMA((4, 4)),
        pltpu.SemaphoreType.DMA((1,)),
    ]
    vmem = pl.BlockSpec(memory_space=pltpu.VMEM)
    hbm = pl.BlockSpec(memory_space=pl.ANY)
    return pl.pallas_call(
        attention_kernel,
        out_shape=(
            jax.ShapeDtypeStruct((T, 3 * HD), BF16),
            jax.ShapeDtypeStruct((3, T, 3 * HD), BF16),
            jax.ShapeDtypeStruct((NX, NZ * NY, 96, T), BF16),
        ),
        in_specs=[vmem, vmem, hbm],
        out_specs=(vmem, vmem, hbm),
        scratch_shapes=scratch,
        compiler_params=pltpu.CompilerParams(
            collective_id=0, has_side_effects=True, vmem_limit_bytes=58 * 2**20
        ),
        cost_estimate=pl.CostEstimate(flops=12 * 10**9, bytes_accessed=4 * 10**6, transcendentals=6 * 10**6),
        name="attention_tile",
    )(projected, cotangent, hidden_t)


def weight_kernel(g_ref, hx_ref, w_ref, dw_ref, dh_ref, gx, dwb, dwr, dhb, dhr, sem_gs, sem_gr, sem_ws, sem_wr, sem_hs, sem_hr):
    z, y, x, t = coords()
    zy = z * NY + y
    me = lax.axis_index("seq")

    def xs(d):
        return (x + d) % NX

    def block(d):
        return (zy + d) % (NZ * NY)

    def ts(d):
        return (t + d) % 4

    barrier = pltpu.get_barrier_semaphore()
    peers = [(zy * NX + xs(d), t) for d in (1, 2, 3)] + [(block(d) * NX + x, t) for d in range(1, 8)]
    peers += [(me, ts(d)) for d in (1, 2, 3)]
    for peer in peers:
        pl.semaphore_signal(barrier, inc=1, device_id=peer, device_id_type=MESH)
    pl.semaphore_wait(barrier, len(peers))

    def send_g(c, d):
        return pltpu.make_async_remote_copy(
            src_ref=g_ref.at[c], dst_ref=gx.at[x, c], send_sem=sem_gs.at[c, d], recv_sem=sem_gr.at[c, d],
            device_id=(zy * NX + xs(d), t), device_id_type=MESH,
        )

    def send_w(c, d):
        return pltpu.make_async_remote_copy(
            src_ref=dwb.at[block(d), c], dst_ref=dwr.at[zy, c], send_sem=sem_ws.at[c, d], recv_sem=sem_wr.at[c, d],
            device_id=(block(d) * NX + x, t), device_id_type=MESH,
        )

    def send_h(d):
        return pltpu.make_async_remote_copy(
            src_ref=dhb.at[ts(d)], dst_ref=dhr.at[t], send_sem=sem_hs.at[d], recv_sem=sem_hr.at[d],
            device_id=(me, ts(d)), device_id_type=MESH,
        )

    for c in range(3):
        for d in (1, 2, 3):
            send_g(c, d).start()
    gx[x] = g_ref[...]

    def hidden_part(d):
        to = ts(d)
        for i in range(3):
            v = 0.0
            for c in range(3):
                rows = pl.ds(pl.multiple_of(to * 768 + i * 256, 256), 256)
                v = v + dot(g_ref[c], w_ref[c, rows, :], NT)
            dhb[to, :, i * 256 : (i + 1) * 256] = v.astype(BF16)

    def hidden_send(d, _):
        hidden_part(d)
        send_h(d).start()
        return 0

    lax.fori_loop(1, 4, hidden_send, 0)
    hidden_part(0)
    dhr[t] = dhb[t]

    for c in range(3):
        for d in (1, 2, 3):
            pltpu.make_async_remote_copy(
                src_ref=g_ref.at[c], dst_ref=gx.at[xs(4 - d), c], send_sem=sem_gs.at[c, d],
                recv_sem=sem_gr.at[c, d], device_id=(zy * NX + xs(d), t), device_id_type=MESH,
            ).wait_recv()

        def rows_of(i, _):
            v = 0.0
            for xx in range(NX):
                h = hx_ref[xx, pl.ds(i * 4, 4)].reshape(4 * 96, T)
                v = v + dot(h, gx[xx, c])
            dwb[pl.ds(i * 4, 4), c] = v.astype(BF16).reshape(4, 96, 384)
            return 0

        lax.fori_loop(0, 2, rows_of, 0)
        for d in range(1, 8):
            send_w(c, d).start()
        dwr[zy, c] = dwb[zy, c]

    for d in (1, 2, 3):
        pltpu.make_async_remote_copy(
            src_ref=dhb.at[0], dst_ref=dhr.at[ts(4 - d)], send_sem=sem_hs.at[d], recv_sem=sem_hr.at[d],
            device_id=(me, ts(d)), device_id_type=MESH,
        ).wait_recv()
    v = dhr[0].astype(F32)
    for i in range(1, 4):
        v = v + dhr[i].astype(F32)
    dh_ref[...] = v.astype(BF16)

    for c in range(3):
        for d in range(1, 8):
            pltpu.make_async_remote_copy(
                src_ref=dwb.at[0, c], dst_ref=dwr.at[block(8 - d), c], send_sem=sem_ws.at[c, d],
                recv_sem=sem_wr.at[c, d], device_id=(block(d) * NX + x, t), device_id_type=MESH,
            ).wait_recv()
        v = dwr[0, c].astype(F32)
        for i in range(1, 8):
            v = v + dwr[i, c].astype(F32)
        dw_ref[c] = v

    for c in range(3):
        for d in (1, 2, 3):
            send_g(c, d).wait_send()
        for d in range(1, 8):
            send_w(c, d).wait_send()
    for d in (1, 2, 3):
        send_h(d).wait_send()


def weight_call(grad_proj, hidden_x, weight):
    vmem = pl.BlockSpec(memory_space=pltpu.VMEM)
    return pl.pallas_call(
        weight_kernel,
        out_shape=(jax.ShapeDtypeStruct((3, 96, 384), F32), jax.ShapeDtypeStruct((T, 768), BF16)),
        in_specs=[vmem] * 3,
        out_specs=(vmem, vmem),
        scratch_shapes=[
            pltpu.VMEM((NX, 3, T, 384), BF16),
            pltpu.VMEM((8, 3, 96, 384), BF16),
            pltpu.VMEM((8, 3, 96, 384), BF16),
            pltpu.VMEM((4, T, 768), BF16),
            pltpu.VMEM((4, T, 768), BF16),
            pltpu.SemaphoreType.DMA((3, 4)),
            pltpu.SemaphoreType.DMA((3, 4)),
            pltpu.SemaphoreType.DMA((3, 8)),
            pltpu.SemaphoreType.DMA((3, 8)),
            pltpu.SemaphoreType.DMA((4,)),
            pltpu.SemaphoreType.DMA((4,)),
        ],
        compiler_params=pltpu.CompilerParams(
            collective_id=1, has_side_effects=True, vmem_limit_bytes=48 * 2**20
        ),
        cost_estimate=pl.CostEstimate(flops=4 * 10**9, bytes_accessed=10 * 10**6, transcendentals=0),
        name="weight_tail",
    )(grad_proj, hidden_x, weight)


def on_device(hidden, qkv_weight, cotangent):
    weight = qkv_weight.transpose(1, 0, 2)
    projected = jnp.einsum("td,cdj->ctj", hidden, weight, preferred_element_type=F32).astype(BF16)
    hidden_t = hidden.T.reshape(NZ * NY, NX, 96, T)
    attention, grad_proj, hidden_x = attention_call(projected, cotangent, hidden_t)
    grad_weight, grad_hidden = weight_call(grad_proj, hidden_x, weight)
    return attention, grad_hidden, grad_weight.transpose(1, 0, 2)


def solution(mesh):
    in_specs = (P("seq", None), P(None, None, "tp"), P("seq", "tp"))
    out_specs = (P("seq", "tp"), P("seq", "tp"), P("seq", None, "tp"))
    return jax.shard_map(
        on_device, mesh=mesh, in_specs=in_specs, out_specs=out_specs, check_vma=False
    )
```

time: 937 us -> 158 us (0.17)
  waiting for transfers between devices: 634 us -> 0 us
  blocking collectives: 157 us -> 0 us
  Pallas kernels: 0 us -> 143 us
  matrix products: 93.8 us -> 6.62 us
  local copies, waits for them, and re-layouts: 23.9 us -> 6.23 us
  between operations: 14.2 us -> 0.67 us
  other arithmetic: 12.8 us -> 0 us
    all_gather x4 -> x0, waiting for transfers between devices: 417 us -> none  [the longest x1 162 us: on_device(): lax.all_gather(key_rows, 'seq', axis=0, tiled=True)]
    unnamed x7 -> x0, waiting for transfers between devices: 197 us -> none
    all_gather x2 -> x0, blocking collectives: 157 us -> none  [the longest x1 81.4 us: on_device(): lax.all_gather(row_delta, 'seq', axis=0, tiled=True)]
    pallas_call x0 -> x2, Pallas kernels: none -> 143 us  [the longest x1 97.8 us: attention_call(): pl.pallas_call(attention_kernel, out_shape=(jax.ShapeDtypeStruct((T, 3 *...]
    dot_general x9 -> x1, matrix products: 93.8 us -> 6.62 us  [on_device(): jnp.einsum('td,cdj->ctj', hidden, weight, preferred_element_type=F32)]
    reduce_scatter x1 -> x0, waiting for transfers between devices: 20.5 us -> none  [on_device(): lax.psum_scatter(hidden_terms, 'tp', scatter_dimension=1, tiled=True)]
    unnamed x13 -> x11, local copies, waits for them, and re-layouts: 20.6 us -> 4.66 us
    reduce_sum x1 -> x0, other arithmetic: 10.9 us -> none  [on_device(): jnp.sum(jnp.exp(scores - top_score), axis=-1, keepdims=True)]
  transfers between devices with their start and end apart: 6 -> 0, of which waited for: 5 -> 0; matrix products, arithmetic and copies ran while one was open for 10% -> 0% of each run, Pallas kernels for 0% -> 0%
where the time goes in v1:
time: 158 us; the launch traced here: 156 us
  Pallas kernels  143 us (91%)
  matrix products  6.62 us (4%)
  local copies, waits for them, and re-layouts  6.23 us (4%)
    pallas_call x1, Pallas kernels, attention_call(): pl.pallas_call(attention_kernel, out_shape=(jax.ShapeDtypeStruct((T, 3 *...  97.8 us
    pallas_call x1, Pallas kernels, weight_call(): pl.pallas_call(weight_kernel, out_shape=(jax.ShapeDtypeStruct((3, 96, 384...  44.9 us
    dot_general x1, matrix products, on_device(): jnp.einsum('td,cdj->ctj', hidden, weight, preferred_element_type=F32)  6.62 us
    unnamed x11, local copies, waits for them, and re-layouts  4.66 us

profile of v1, /device:TPU:16, one launch (start us, length us, event | category | flops | bytes accessed | tf_op | source)
XLA Modules:
  0.0 156.3 jit_solution(15147825001609439777)
XLA Ops:
  0.6 0.0 copy-start.2
  0.6 6.6 %fusion.5.p_ref = bf16[3,256,384]{2,1,0:T(8,128)(2,1)} fusion(bf16[256,3072]{1,0:T(8,128)(2,1)} %param.3, bf16[3072,3,384]{2,0,1:T(8,128)(2,1)} %param.4), kind=kOutput, calls=%fused_computation.3 | convolution fusion | flops 1812234240 | bytes 9240576 | tf_op jit(solution)/shard_map/td,cdj->ctj/dot_general | solution.py:506
  7.3 0.0 copy-done.2
  7.3 1.6 %copy.8 = bf16[3072,256]{1,0:T(8,128)(2,1)} copy(bf16[3072,256]{0,1:T(8,128)(2,1)S(1)} %bitcast.16) | data formatting | bytes 3145728 | tf_op jit(solution)/shard_map/transpose | solution.py:507
  8.8 97.8 %attention_tile.1 = (bf16[256,384]{1,0:T(8,128)(2,1)}, bf16[3,256,384]{2,1,0:T(8,128)(2,1)}, bf16[4,8,96,256]{3,2,1,0:T(8,128)(2,1)}) custom-call(bf16[3,256,384]{2,1,0:T(8,128)(2,1)} %fusion.5.p_ref, bf16[256,384]{1,0:T(8,128)(2,1)} %cot_ref.1, bf16[8,4,96,256]{3,2,1,0:T(8,128)(2,1)} %bitcast.17), custom_call_target="tpu_custom_call" | custom-call | flops 12000000000 | bytes 4000000 | tf_op jit(solution)/shard_map/attention_tile/pallas_call | solution.py:346
  106.6 0.0 copy-start
  106.7 1.4 copy-done
  108.1 0.0 copy-start.1
  108.1 1.1 copy-done.1
  109.1 0.0 copy-start.3
  109.1 44.9 %weight_tail.1 = (f32[3,96,384]{2,1,0:T(8,128)S(1)}, bf16[256,768]{1,0:T(8,128)(2,1)S(1)}) custom-call(bf16[3,256,384]{2,1,0:T(8,128)(2,1)S(1)} %copy-done.1, bf16[4,8,96,256]{3,2,1,0:T(8,128)(2,1)S(1)} %copy-done, bf16[3,3072,384]{2,1,0:T(8,128)(2,1)} %bitcast.18), custom_call_target="tpu_custom_call" | custom-call | flops 4000000000 | bytes 10000000 | tf_op jit(solution)/shard_map/weight_tail/pallas_call | solution.py:478
  154.1 0.0 copy-done.3
  154.1 0.7 copy.14
  154.7 0.7 copy.15
  155.5 0.8 copy.16
Async XLA Ops:
  0.6 6.6 %copy-start.2 = (bf16[256,3072]{1,0:T(8,128)(2,1)S(1)}, bf16[256,3072]{1,0:T(8,128)(2,1)}, u32[]{:S(2)}) copy-start(bf16[256,3072]{1,0:T(8,128)(2,1)} %param.3) | copy-start | bytes 4718596
  106.6 1.4 copy-start
  108.1 1.1 copy-start.1
  109.1 44.9 %copy-start.3 = (bf16[256,384]{1,0:T(8,128)(2,1)S(1)}, bf16[256,384]{1,0:T(8,128)(2,1)}, u32[]{:S(2)}) copy-start(bf16[256,384]{1,0:T(8,128)(2,1)} %get-tuple-element.16) | copy-start | bytes 589828

commit v2 on v0

v2 whole, which is shorter than its diff:
```python
import math

import jax
import jax.numpy as jnp
from jax import lax
from jax.experimental import pallas as pl
from jax.experimental.pallas import tpu as pltpu
from jax.sharding import PartitionSpec as P

HD = 128
T = 256
NZ, NY, NX = 4, 2, 4
KEYS = NZ * NY * T
CHUNK = 512
SCALE = 1.0 / math.sqrt(HD)
LOG2 = SCALE * math.log2(math.e)
MESH = pl.DeviceIdType.MESH
F32, BF16 = jnp.float32, jnp.bfloat16
NN = (((1,), (0,)), ((), ()))
NT = (((1,), (1,)), ((), ()))


def dot(a, b, dims=NN):
    return lax.dot_general(a, b, dims, preferred_element_type=F32)


def coords():
    s = lax.axis_index("seq")
    return s // (NY * NX), (s // NX) % NY, s % NX, lax.axis_index("tp")


def seq_of(z, y, x):
    return (z * NY + y) * NX + x


def aligned(i, n):
    return pl.ds(pl.multiple_of(i * n, n), n)

Y_QG, Y_KVA, Y_KV1 = 0, 1, 2
X_QGA, X_QGR, X_QG1 = 3, 7, 11
Z_KVA, Z_KVAR, Z_KV1, Z_KV1R = 15, 19, 23, 27
X_HX, C_HX, X_STA, X_ST1 = 31, 35, 39, 43
X_GA0, X_GA1, X_GH = 47, 51, 55
C_DH, H_DH, N_SEM = 59, 61, 62
RING = (1, 2, 3)


def kernel(
    hidden_ref, w_ref, cot_ref, att_ref, dw_ref, dh_ref,
    h_v, w_v, cot_v, own_qg, own_kv, ht, hx, qg, kv, vkt, pt, ut, s_buf, st, sm, sm_all, ma, cs, es, rhs,
    ob, ro, kb, rk, gx_a, gx_h, dwb_a, dwr_a, dwb_h, dwr_h, dhb, dhc, dhs, dhr,
    sem_l, sem_s, sem_r, sem_os, sem_or, sem_ks, sem_kr, sem_ws, sem_wr,
):
    z, y, x, t = coords()
    other = 1 - y
    core = t % 2
    mate = t + 1 - 2 * core
    across = (t + 2) % 4
    me = lax.axis_index("seq")
    head_a, head_b = 2 * y, 2 - 2 * y
    zy = z * NY + y

    def at(zz, yy, xx):
        return (seq_of(zz, yy, xx), t)

    def xs(d):
        return (x + d) % NX

    def zs(d):
        return (z + d) % NZ

    local = [
        pltpu.make_async_copy(hidden_ref, h_v, sem_l.at[0]),
        pltpu.make_async_copy(w_ref.at[1], w_v.at[1], sem_l.at[1]),
        pltpu.make_async_copy(w_ref.at[2], w_v.at[2], sem_l.at[2]),
        pltpu.make_async_copy(w_ref.at[0], w_v.at[0], sem_l.at[3]),
        pltpu.make_async_copy(cot_ref, cot_v, sem_l.at[4]),
    ]
    for c in local:
        c.start()

    barrier = pltpu.get_barrier_semaphore()
    peers = [at(z, y, xs(d)) for d in RING] + [at(z, other, xs(d)) for d in range(4)]
    peers += [at(zs(d), y, x) for d in RING] + [at(zs(d), other, x) for d in RING]
    peers += [(me, mate), (me, across)]
    for peer in peers:
        pl.semaphore_signal(barrier, inc=1, device_id=peer, device_id_type=MESH)
    pl.semaphore_wait(barrier, len(peers))

    def remote(i, src, dst, peer):
        return pltpu.make_async_remote_copy(
            src_ref=src, dst_ref=dst, send_sem=sem_s.at[i], recv_sem=sem_r.at[i],
            device_id=peer, device_id_type=MESH,
        )

    sent = []

    def send(i, src, dst, peer):
        sent.append(remote(i, src, dst, peer))
        sent[-1].start()

    def got(i, dst):
        remote(i, dst, dst, (me, mate)).wait_recv()

    def qg_slot(yy, xx):
        return qg.at[4 + yy * NX + xx]

    def kv_rows(j, yy, zz):
        return kv.at[j, :, aligned(yy * NZ + zz, T), :]

    def columns(c, h):
        return w_v[c, :, aligned(h, HD)]

    def project_kv(h):
        v = dot(h_v[...], jnp.concatenate([columns(1, h), columns(2, h)], axis=1))
        own_kv[h, 0] = v[:, :HD].astype(BF16)
        own_kv[h, 1] = v[:, HD:].astype(BF16)

    partner = at(z, other, x)
    for c in local[:3]:
        c.wait()
    project_kv(head_b)
    send(Y_KVA, own_kv.at[head_b], kv_rows(1, y, z), partner)
    project_kv(head_a)
    for d in RING:
        send(Z_KVA + d, own_kv.at[head_a], kv_rows(1, y, z), at(zs(d), y, x))
    kv[1, :, aligned(y * NZ + z, T), :] = own_kv[head_a]
    for c in local[3:]:
        c.wait()
    for h in range(3):
        own_qg[h, 1] = cot_v[:, h * HD : (h + 1) * HD]
    v = dot(h_v[...], jnp.concatenate([columns(0, head_b), columns(0, head_a)], axis=1))
    own_qg[head_b, 0] = v[:, :HD].astype(BF16)
    own_qg[head_a, 0] = v[:, HD:].astype(BF16)
    send(Y_QG, own_qg.at[head_b], qg_slot(y, x), partner)
    for d in RING:
        send(X_QGA + d, own_qg.at[head_a], qg_slot(y, x), at(z, y, xs(d)))
    qg[4 + y * NX + x] = own_qg[head_a]

    got(Y_KVA, kv_rows(1, other, z))
    for d in RING:
        send(Z_KVAR + d, kv_rows(1, other, z), kv_rows(1, other, z), at(zs(d), y, x))
    project_kv(1)
    own_qg[1, 0] = dot(h_v[...], columns(0, 1)).astype(BF16)
    got(Y_QG, qg_slot(other, x))
    for d in RING:
        send(X_QGR + d, qg_slot(other, x), qg_slot(other, x), at(z, y, xs(d)))
    qg[x] = own_qg[1]
    kv[0, :, aligned(y * NZ + z, T), :] = own_kv[1]
    sm[...] = jnp.zeros_like(sm)
    ma[...] = jnp.zeros_like(ma)

    def hidden_rows(i, _):
        ht[i] = h_v[:, aligned(i, 384)].T.reshape(NX, 96, T)
        return 0

    lax.fori_loop(0, NZ * NY, hidden_rows, 0)
    hx[x] = ht[:, x]

    def transpose_block(j, yy, zz):
        i = yy * NZ + zz
        vkt[0:HD, aligned(i, T)] = kv[j, 1, aligned(i, T), :].T
        vkt[HD : 2 * HD, aligned(i, T)] = kv[j, 0, aligned(i, T), :].T

    def transpose_keys(j, base, base_relay):
        transpose_block(j, y, z)
        transpose_block(j, other, z)

        def step(d, _):
            got(base + d, kv_rows(j, y, zs(4 - d)))
            transpose_block(j, y, zs(4 - d))
            got(base_relay + d, kv_rows(j, other, zs(4 - d)))
            transpose_block(j, other, zs(4 - d))
            return 0

        lax.fori_loop(1, 4, step, 0)

    transpose_keys(1, Z_KVA, Z_KVAR)

    send(Y_KV1, own_kv.at[1], kv_rows(0, y, z), partner)
    half = pl.ds(4 * core, 4)
    for d in RING:
        send(Z_KV1 + d, own_kv.at[1], kv_rows(0, y, z), at(zs(d), y, x))
        send(X_HX + d, ht.at[half, xs(d)], hx.at[x, half], at(z, y, xs(d)))
    for d in RING:
        send(X_QG1 + d, own_qg.at[1], qg.at[x], at(z, y, xs(d)))

    chunks = [slice(c * CHUNK, (c + 1) * CHUNK) for c in range(KEYS // CHUNK)]

    def unit(j, q_slot, slot, row):
        q, g = qg[q_slot, 0], qg[q_slot, 1]
        top = None
        for c in chunks:
            s = dot(kv[j, 0, c, :], q, NT)
            s_buf[c] = s
            m = jnp.max(s, axis=0, keepdims=True)
            top = m if top is None else jnp.maximum(top, m)
        top = top * LOG2
        total, out = 0.0, 0.0
        for c in chunks:
            p = jnp.exp2(s_buf[c] * LOG2 - top)
            total = total + jnp.sum(p, axis=0, keepdims=True)
            p = p.astype(BF16)
            pt[slot, c, :] = p
            out = out + dot(vkt[:, c], p)
        g_t = g.astype(F32).T
        delta = jnp.sum(g_t * out[:HD], axis=0, keepdims=True) / total
        grad = 0.0
        for c in chunks:
            dp = dot(kv[j, 1, c, :], g, NT)
            d = (pt[slot, c, :].astype(F32) * (dp - delta)).astype(BF16)
            ut[slot, c, :] = d
            grad = grad + dot(vkt[HD:, c], d)
        st[slot, : 2 * HD] = out
        st[slot, 2 * HD :] = grad
        sm[j, 0, pl.ds(row, 1), :] = top + jnp.log2(total)
        sm[j, 1, pl.ds(row, 1), :] = delta
        ma[j, pl.ds(row, 1), :] = top

    def row_a(i):
        yy = (y + i // 4) % 2
        return yy, xs(4 - i % 4), yy * NX + xs(4 - i % 4)

    def relay_shared():
        rows = kv_rows(0, other, z)
        return [remote(Z_KV1R + d, rows, rows, at(zs(d), y, x)) for d in RING]

    def unit_a(i, _):
        _, _, r = row_a(i)

        @pl.when(i % 4 != 0)
        def _():
            got(X_QGA + i, qg.at[4 + r])

        @pl.when(i == 4)
        def _():
            got(Y_KV1, kv_rows(0, other, z))
            for c in relay_shared():
                c.start()

        unit(1, 4 + r, r, r)
        return 0

    lax.fori_loop(0, 8, unit_a, 0)
    sent.extend(relay_shared())

    def send_stats(j, base):
        for d in RING:
            send(base + d, sm.at[j], sm_all.at[j, x], at(z, y, xs(d)))
        sm_all[j, x] = sm[j]

    def combine(j, base):
        for d in RING:
            got(base + d, sm_all.at[j, xs(4 - d)])
        lse = sm_all[j, :, 0]
        top = jnp.max(lse, axis=0)
        lse_all = top + jnp.log2(jnp.sum(jnp.exp2(lse - top), axis=0))
        delta = jnp.sum(jnp.exp2(lse - lse_all) * sm_all[j, :, 1], axis=0)
        cs[j] = jnp.exp2(ma[j] - lse_all)
        es[j] = delta - sm[j, 1]

    send_stats(1, X_STA)
    for d in RING:
        part = hx.at[xs(4 - d), half]
        got(X_HX + d, part)
        send(C_HX + d, part, part, (me, mate))
    transpose_keys(0, Z_KV1, Z_KV1R)
    unit(0, x, 8, x)
    combine(1, X_STA)

    def prepare(j, row, slot, q_slot, r, b):
        c, e = cs[j, pl.ds(row, 1), :], es[j, pl.ds(row, 1), :]
        o = st[slot, 0:HD] * c
        dq = (st[slot, 2 * HD :] - e * st[slot, HD : 2 * HD]) * (c * SCALE)
        ob[b, 0] = o.T.astype(BF16)
        ob[b, 1] = dq.T.astype(BF16)
        cols = jnp.concatenate([c, e, jnp.zeros((6, T), F32)], axis=0).T
        c, e = cols[:, 0:1], cols[:, 1:2]
        cq = c * qg[q_slot, 0].astype(F32)
        rhs[r, :, 0:HD] = (c * qg[q_slot, 1].astype(F32)).astype(BF16)
        rhs[r, :, HD : 2 * HD] = (e * cq).astype(BF16)
        rhs[r, :, 2 * HD :] = cq.astype(BF16)

    def copy_o(kind, d, b, h, peer):
        return pltpu.make_async_remote_copy(
            src_ref=ob.at[b], dst_ref=ro.at[h, x], send_sem=sem_os.at[kind, d], recv_sem=sem_or.at[kind, d],
            device_id=peer, device_id_type=MESH,
        )

    def got_o(kind, d, h):
        pltpu.make_async_remote_copy(
            src_ref=ob.at[0], dst_ref=ro.at[h, xs(d)], send_sem=sem_os.at[kind, d], recv_sem=sem_or.at[kind, d],
            device_id=partner, device_id_type=MESH,
        ).wait_recv()

    def send_a(i):
        yy, xx, r = row_a(i)
        return copy_o(i // 4, i % 4, 4 + r, head_a, at(z, yy, xx))

    def prepare_a(k, _):
        i = 7 - k
        _, _, r = row_a(i)
        prepare(1, r, r, 4 + r, r, 4 + r)

        @pl.when(i != 0)
        def _():
            send_a(i).start()

        return 0

    lax.fori_loop(0, 8, prepare_a, 0)
    ro[head_a, x] = ob[4 + y * NX + x]

    def copy_k(j, own, d):
        yy = y if own else other
        zz = zs(d)
        kind = 2 * j + (0 if own else 1)
        b = j * 8 + yy * NZ + zz
        return pltpu.make_async_remote_copy(
            src_ref=kb.at[b], dst_ref=rk.at[j * 8 + y * NZ + z], send_sem=sem_ks.at[kind, d],
            recv_sem=sem_kr.at[kind, d], device_id=at(zz, yy, x), device_id_type=MESH,
        )

    def got_k(j, own, d):
        kind = 2 * j + (0 if own else 1)
        yy = y if own else other
        pltpu.make_async_remote_copy(
            src_ref=kb.at[0], dst_ref=rk.at[j * 8 + yy * NZ + zs(4 - d)], send_sem=sem_ks.at[kind, d],
            recv_sem=sem_kr.at[kind, d], device_id=partner, device_id_type=MESH,
        ).wait_recv()

    def key_block(j, i):
        slots = (8, 0, 1, 2) if j == 0 else range(8)
        rows = aligned(i, T)
        dv = dk = 0.0
        for r, slot in enumerate(slots):
            dv = dv + dot(pt[slot, rows, :], rhs[r, :, : 2 * HD])
            dk = dk + dot(ut[slot, rows, :], rhs[r, :, 2 * HD :])
        kb[j * 8 + i, 0] = ((dk - dv[:, HD:]) * SCALE).astype(BF16)
        kb[j * 8 + i, 1] = dv[:, :HD].astype(BF16)

    def loop(first, last, step):
        def body(i, _):
            step(i)
            return 0

        lax.fori_loop(first, last, body, 0)

    def key_blocks(j):
        def step(k):
            d = (k + 1) % 4
            yy = (other + k // 4) % 2
            key_block(j, yy * NZ + zs(d))

            @pl.when(k < 4)
            def _():
                copy_k(j, False, d).start()

            @pl.when((k >= 4) & (k < 7))
            def _():
                copy_k(j, True, d).start()

        loop(0, 8, step)
        rk[j * 8 + y * NZ + z] = kb[j * 8 + y * NZ + z]

    key_blocks(1)

    def unit_shared(d, _):
        got(X_QG1 + d, qg.at[xs(4 - d)])
        unit(0, xs(4 - d), d - 1, xs(4 - d))
        return 0

    lax.fori_loop(1, 4, unit_shared, 0)
    send_stats(0, X_ST1)

    def total_o(h, part):
        v = ro[h, 0, part].astype(F32)
        for xx in range(1, NX):
            v = v + ro[h, xx, part].astype(F32)
        return v.astype(BF16)

    def total_k(slots, part):
        v = 0.0
        for i in slots:
            v = v + rk[i, part].astype(F32)
        return v.astype(BF16)

    loop(1, 4, lambda d: got_o(0, d, head_a))
    loop(0, 4, lambda d: got_o(1, d, head_b))
    for i, h in enumerate((0, 2)):
        att_ref[:, h * HD : (h + 1) * HD] = total_o(h, 0)
        gx_a[x, 0, :, i * HD : (i + 1) * HD] = total_o(h, 1)
    for d in RING:
        send(X_GA0 + d, gx_a.at[x, 0], gx_a.at[x, 0], at(z, y, xs(d)))
    loop(1, 4, lambda d: got_k(1, True, d))
    loop(0, 4, lambda d: got_k(1, False, d))
    for i, slots in enumerate((range(8, 12), range(12, 16))):
        for part in (0, 1):
            gx_a[x, 1 + part, :, i * HD : (i + 1) * HD] = total_k(slots, part)
    for d in RING:
        send(X_GA1 + d, gx_a.at[x, pl.ds(1, 2)], gx_a.at[x, pl.ds(1, 2)], at(z, y, xs(d)))

    combine(0, X_ST1)

    def send_shared(d):
        return copy_o(2, d, xs(4 - d), 1, at(z, y, xs(4 - d)))

    def prepare_shared(d):
        slot = (d + 8) % 9
        prepare(0, xs(4 - d), slot, xs(4 - d), d, xs(4 - d))

        @pl.when(d != 0)
        def _():
            send_shared(d).start()

    loop(0, 4, prepare_shared)
    ro[1, x] = ob[x]
    key_blocks(0)

    def block(d):
        return (zy + d) % (NZ * NY)

    def copy_w(c, d):
        src, dst = (dwb_h.at[block(d)], dwr_h.at[zy]) if c == 3 else (dwb_a.at[block(d), c], dwr_a.at[zy, c])
        return pltpu.make_async_remote_copy(
            src_ref=src, dst_ref=dst, send_sem=sem_ws.at[c, d], recv_sem=sem_wr.at[c, d],
            device_id=(block(d) * NX + x, t), device_id_type=MESH,
        )

    def got_w(c, d):
        dst = dwr_h.at[block(8 - d)] if c == 3 else dwr_a.at[block(8 - d), c]
        pltpu.make_async_remote_copy(
            src_ref=dst, dst_ref=dst, send_sem=sem_ws.at[c, d], recv_sem=sem_wr.at[c, d],
            device_id=partner, device_id_type=MESH,
        ).wait_recv()

    def weight_rows(gx, dwb, c):
        def step(i):
            v = 0.0
            for xx in range(NX):
                v = v + dot(hx[xx, pl.ds(i * 4, 4)].reshape(4 * 96, T), gx[xx, c])
            dwb[pl.ds(i * 4, 4), c] = v.astype(BF16).reshape(4, 96, v.shape[1])

        loop(0, 2, step)

    for d in RING:
        got(C_HX + d, hx.at[xs(4 - d), pl.ds(4 - 4 * core, 4)])
        got(X_GA0 + d, gx_a.at[xs(4 - d), 0])
    for c in range(3):
        if c == 1:
            for d in RING:
                got(X_GA1 + d, gx_a.at[xs(4 - d), pl.ds(1, 2)])
        weight_rows(gx_a, dwb_a, c)
        loop(1, 8, lambda d, c=c: copy_w(c, d).start())
        dwr_a[zy, c] = dwb_a[zy, c]

    loop(1, 4, lambda d: got_o(2, d, 1))
    att_ref[:, HD : 2 * HD] = total_o(1, 0)
    gx_h[x, 0] = total_o(1, 1)
    loop(1, 4, lambda d: got_k(0, True, d))
    loop(0, 4, lambda d: got_k(0, False, d))
    for part in (0, 1):
        gx_h[x, 1 + part] = total_k(range(8), part)
    for d in RING:
        send(X_GH + d, gx_h.at[x], gx_h.at[x], at(z, y, xs(d)))

    def hidden_part(to):
        for i in range(3):
            v = 0.0
            for c in range(3):
                g = jnp.concatenate([gx_a[x, c, :, :HD], gx_h[x, c], gx_a[x, c, :, HD:]], axis=1)
                rows = pl.ds(pl.multiple_of(to * 768 + i * 256, 256), 256)
                v = v + dot(g, w_v[c, rows, :], NT)
            dhb[to, :, i * 256 : (i + 1) * 256] = v.astype(BF16)

    def hidden_mate(i):
        hidden_part(2 * i + 1 - core)
        copy_mate(i).start()

    def copy_mate(i):
        return remote(C_DH + i, dhb.at[2 * i + 1 - core], dhc.at[i], (me, mate))

    loop(0, 2, hidden_mate)
    loop(0, 2, lambda i: hidden_part(2 * i + core))
    for i in range(2):
        sent.append(copy_mate(i))
        got(C_DH + i, dhc.at[i])
    hi = t // 2
    dhs[...] = (dhb[across].astype(F32) + dhc[1 - hi].astype(F32)).astype(BF16)
    send(H_DH, dhs, dhr, (me, across))

    for d in RING:
        got(X_GH + d, gx_h.at[xs(4 - d)])
    for c in range(3):
        weight_rows(gx_h, dwb_h, c)
    loop(1, 8, lambda d: copy_w(3, d).start())
    dwr_h[zy] = dwb_h[zy]

    for c in range(3):
        loop(1, 8, lambda d, c=c: got_w(c, d))
        v = dwr_a[0, c].astype(F32)
        for i in range(1, 8):
            v = v + dwr_a[i, c].astype(F32)
        dw_ref[c, :, :HD] = v[:, :HD]
        dw_ref[c, :, 2 * HD :] = v[:, HD:]
    loop(1, 8, lambda d: got_w(3, d))
    for c in range(3):
        v = dwr_h[0, c].astype(F32)
        for i in range(1, 8):
            v = v + dwr_h[i, c].astype(F32)
        dw_ref[c, :, HD : 2 * HD] = v
    got(H_DH, dhr)
    dh_ref[...] = (dhb[t].astype(F32) + dhc[hi].astype(F32) + dhr[...].astype(F32)).astype(BF16)

    for c in sent:
        c.wait_send()
    loop(1, 8, lambda i: send_a(i).wait_send())
    loop(1, 4, lambda d: send_shared(d).wait_send())
    for j in (0, 1):
        loop(0, 4, lambda d, j=j: copy_k(j, False, d).wait_send())
        loop(1, 4, lambda d, j=j: copy_k(j, True, d).wait_send())
    for c in range(4):
        loop(1, 8, lambda d, c=c: copy_w(c, d).wait_send())


def call(hidden, weight, cotangent):
    block = (2, T, HD)
    scratch = [
        ((T, 3072), BF16),
        ((3, 3072, 384), BF16),
        ((T, 3 * HD), BF16),
        ((3,) + block, BF16),
        ((3,) + block, BF16),
        ((8, NX, 96, T), BF16),
        ((NX, 8, 96, T), BF16),
        ((12,) + block, BF16),
        ((2, 2, KEYS, HD), BF16),
        ((2 * HD, KEYS), BF16),
        ((9, KEYS, T), BF16),
        ((9, KEYS, T), BF16),
        ((KEYS, T), F32),
        ((9, 3 * HD, T), F32),
        ((2, 2, 8, T), F32),
        ((2, NX, 2, 8, T), F32),
        ((2, 8, T), F32),
        ((2, 8, T), F32),
        ((2, 8, T), F32),
        ((8, T, 3 * HD), BF16),
        ((12,) + block, BF16),
        ((3, NX) + block, BF16),
        ((16,) + block, BF16),
        ((16,) + block, BF16),
        ((NX, 3, T, 2 * HD), BF16),
        ((NX, 3, T, HD), BF16),
        ((8, 3, 96, 2 * HD), BF16),
        ((8, 3, 96, 2 * HD), BF16),
        ((8, 3, 96, HD), BF16),
        ((8, 3, 96, HD), BF16),
        ((4, T, 768), BF16),
        ((2, T, 768), BF16),
        ((T, 768), BF16),
        ((T, 768), BF16),
    ]
    sems = [(5,), (N_SEM,), (N_SEM,), (3, 4), (3, 4), (4, 4), (4, 4), (4, 8), (4, 8)]
    vmem = pl.BlockSpec(memory_space=pltpu.VMEM)
    hbm = pl.BlockSpec(memory_space=pl.ANY)
    return pl.pallas_call(
        kernel,
        out_shape=(
            jax.ShapeDtypeStruct((T, 3 * HD), BF16),
            jax.ShapeDtypeStruct((3, 96, 384), F32),
            jax.ShapeDtypeStruct((T, 768), BF16),
        ),
        in_specs=[hbm] * 3,
        out_specs=(vmem,) * 3,
        scratch_shapes=[pltpu.VMEM(*s) for s in scratch] + [pltpu.SemaphoreType.DMA(s) for s in sems],
        compiler_params=pltpu.CompilerParams(
            collective_id=0, has_side_effects=True, vmem_limit_bytes=63 * 2**20
        ),
        cost_estimate=pl.CostEstimate(flops=18 * 10**9, bytes_accessed=10**7, transcendentals=6 * 10**6),
        name="attention_with_gradients",
    )(hidden, weight, cotangent)


def on_device(hidden, qkv_weight, cotangent):
    attention, grad_weight, grad_hidden = call(hidden, qkv_weight.transpose(1, 0, 2), cotangent)
    return attention, grad_hidden, grad_weight.transpose(1, 0, 2)


def solution(mesh):
    in_specs = (P("seq", None), P(None, None, "tp"), P("seq", "tp"))
    out_specs = (P("seq", "tp"), P("seq", "tp"), P("seq", None, "tp"))
    return jax.shard_map(
        on_device, mesh=mesh, in_specs=in_specs, out_specs=out_specs, check_vma=False
    )
```

time: 937 us -> 118 us (0.13)
  waiting for transfers between devices: 634 us -> 0 us
  blocking collectives: 157 us -> 0 us
  Pallas kernels: 0 us -> 112 us
  matrix products: 93.8 us -> 0 us
  local copies, waits for them, and re-layouts: 23.9 us -> 5.19 us
  between operations: 14.2 us -> 0.64 us
  other arithmetic: 12.8 us -> 0 us
    all_gather x4 -> x0, waiting for transfers between devices: 417 us -> none  [the longest x1 162 us: on_device(): lax.all_gather(key_rows, 'seq', axis=0, tiled=True)]
    unnamed x7 -> x0, waiting for transfers between devices: 197 us -> none
    all_gather x2 -> x0, blocking collectives: 157 us -> none  [the longest x1 81.4 us: on_device(): lax.all_gather(row_delta, 'seq', axis=0, tiled=True)]
    pallas_call x0 -> x1, Pallas kernels: none -> 112 us  [call(): pl.pallas_call(kernel, out_shape=(jax.ShapeDtypeStruct((T, 3 * HD), BF16)...]
    dot_general x9 -> x0, matrix products: 93.8 us -> none  [the longest x1 14.9 us: on_device(): jnp.einsum('hqk,khd->qhd', grad_scores, keys_all, preferred_element_type=...]
    reduce_scatter x1 -> x0, waiting for transfers between devices: 20.5 us -> none  [on_device(): lax.psum_scatter(hidden_terms, 'tp', scatter_dimension=1, tiled=True)]
    unnamed x13 -> x3, local copies, waits for them, and re-layouts: 20.6 us -> 5.19 us
    reduce_sum x1 -> x0, other arithmetic: 10.9 us -> none  [on_device(): jnp.sum(jnp.exp(scores - top_score), axis=-1, keepdims=True)]
  transfers between devices with their start and end apart: 6 -> 0, of which waited for: 5 -> 0; matrix products, arithmetic and copies ran while one was open for 10% -> 0% of each run, Pallas kernels for 0% -> 0%
where the time goes in v2:
time: 118 us
  Pallas kernels  112 us (95%)
  local copies, waits for them, and re-layouts  5.19 us (4%)
    pallas_call x1, Pallas kernels, call(): pl.pallas_call(kernel, out_shape=(jax.ShapeDtypeStruct((T, 3 * HD), BF16)...  112 us
    unnamed x3, local copies, waits for them, and re-layouts  5.19 us

profile of v2, /device:TPU:16, one launch (start us, length us, event | category | flops | bytes accessed | tf_op | source)
XLA Modules:
  0.0 117.6 jit_solution(6730156745916798105)
XLA Ops:
  0.6 111.8 %attention_with_gradients.1 = (bf16[256,384]{1,0:T(8,128)(2,1)}, f32[3,96,384]{2,1,0:T(8,128)}, bf16[256,768]{1,0:T(8,128)(2,1)}) custom-call(bf16[256,3072]{1,0:T(8,128)(2,1)} %hidden_ref.1, bf16[3,3072,384]{2,1,0:T(8,128)(2,1)} %bitcast.3, bf16[256,384]{1,0:T(8,128)(2,1)} %cot_ref.1), custom_call_target="tpu_custom_call" | custom-call | flops 17999998976 | bytes 10000000 | tf_op jit(solution)/shard_map/attention_with_gradients/pallas_call | solution.py:567
  112.4 1.6 %copy.9 = bf16[256,384]{1,0:T(8,128)(2,1)} copy(bf16[256,384]{1,0:T(8,128)(2,1)} %get-tuple-element.12) | data formatting | bytes 393216
  114.0 1.8 %copy.10 = bf16[256,768]{1,0:T(8,128)(2,1)} copy(bf16[256,768]{1,0:T(8,128)(2,1)} %get-tuple-element.13) | data formatting | bytes 786432
  115.8 1.8 %copy.11 = f32[96,3,384]{2,0,1:T(8,128)} copy(f32[96,3,384]{2,0,1:T(8,128)} %bitcast.2) | data formatting | bytes 884736

commit v3 on v2

v3 whole, which is shorter than its diff:
```python
import math

import jax
import jax.numpy as jnp
from jax import lax
from jax.experimental import pallas as pl
from jax.experimental.pallas import tpu as pltpu
from jax.sharding import PartitionSpec as P

HD = 128
T = 256
NZ, NY, NX = 4, 2, 4
KEYS = NZ * NY * T
CHUNK = 512
SCALE = 1.0 / math.sqrt(HD)
LOG2 = SCALE * math.log2(math.e)
MESH = pl.DeviceIdType.MESH
F32, BF16 = jnp.float32, jnp.bfloat16
NN = (((1,), (0,)), ((), ()))
NT = (((1,), (1,)), ((), ()))


def dot(a, b, dims=NN):
    return lax.dot_general(a, b, dims, preferred_element_type=F32)


def coords():
    s = lax.axis_index("seq")
    return s // (NY * NX), (s // NX) % NY, s % NX, lax.axis_index("tp")


def seq_of(z, y, x):
    return (z * NY + y) * NX + x


def aligned(i, n):
    return pl.ds(pl.multiple_of(i * n, n), n)

Y_QG, Y_KVA, Y_KV1 = 0, 1, 2
X_QGA, X_QGR, X_QG1 = 3, 7, 11
Z_KVA, Z_KVAR, Z_KV1, Z_KV1R = 15, 19, 23, 27
X_HX, C_HX, X_STA, X_ST1 = 31, 35, 39, 43
X_GA, X_GHV, X_GHK, X_GHQ = 47, 51, 55, 67
C_DH, H_DH = 59, 61
Y_OA, Y_KA, Y_V1, Y_K1, Y_WA, Y_W1 = 62, 63, 64, 65, 66, 67
X_GB, X_GC, X_GD, N_SEM = 71, 75, 79, 83
RING = (1, 2, 3)


def kernel(
    hidden_ref, w_ref, cot_ref, att_ref, dw_ref, dh_ref,
    h_v, w_v, cot_v, far_qg, far_kv, ht, hx, qg, kv, vkt, pt, ut, s_buf, top_buf, st, sm, sm_all, ma, cs, es, rhs,
    ob, ro, kb, rk, ya_s, ya_r, y1_s, y1_r, ywa_s, ywa_r, yw1_s, yw1_r,
    gx_a, gx_h, dwb_a, dwr_a, dwb_h, dwr_h, dhc, dhr,
    sem_l, sem_s, sem_r, sem_os, sem_or, sem_ks, sem_kr, sem_ws, sem_wr,
):
    z, y, x, t = coords()
    other = 1 - y
    core = t % 2
    mate = t + 1 - 2 * core
    across = (t + 2) % 4
    me = lax.axis_index("seq")
    head_a, head_b = 2 * y, 2 - 2 * y

    def at(zz, yy, xx):
        return (seq_of(zz, yy, xx), t)

    def xs(d):
        return (x + d) % NX

    def zs(d):
        return (z + d) % NZ

    local = [
        pltpu.make_async_copy(hidden_ref, h_v, sem_l.at[0]),
        pltpu.make_async_copy(w_ref.at[1], w_v.at[1], sem_l.at[1]),
        pltpu.make_async_copy(w_ref.at[2], w_v.at[2], sem_l.at[2]),
        pltpu.make_async_copy(w_ref.at[0], w_v.at[0], sem_l.at[3]),
        pltpu.make_async_copy(cot_ref, cot_v, sem_l.at[4]),
    ]
    for c in local:
        c.start()

    barrier = pltpu.get_barrier_semaphore()
    peers = [at(z, y, xs(d)) for d in RING] + [at(zs(d), y, x) for d in RING]
    peers += [at(z, other, x), (me, mate), (me, across)]
    for peer in peers:
        pl.semaphore_signal(barrier, inc=1, device_id=peer, device_id_type=MESH)
    pl.semaphore_wait(barrier, len(peers))

    def remote(i, src, dst, peer):
        return pltpu.make_async_remote_copy(
            src_ref=src, dst_ref=dst, send_sem=sem_s.at[i], recv_sem=sem_r.at[i],
            device_id=peer, device_id_type=MESH,
        )

    sent = []

    def send(i, src, dst, peer):
        sent.append(remote(i, src, dst, peer))
        sent[-1].start()

    def got(i, dst):
        remote(i, dst, dst, (me, mate)).wait_recv()

    def qg_slot(yy, xx):
        return qg.at[4 + yy * NX + xx]

    def kv_rows(j, yy, zz):
        return kv.at[j, :, aligned(yy * NZ + zz, T), :]

    def columns(c, h):
        return w_v[c, :, aligned(h, HD)]

    def project_kv(h, dst):
        v = dot(h_v[...], jnp.concatenate([columns(1, h), columns(2, h)], axis=1))
        dst[0] = v[:, :HD].astype(BF16)
        dst[1] = v[:, HD:].astype(BF16)

    partner = at(z, other, x)
    own_a, own_1 = qg_slot(y, x), qg.at[x]
    keys_a, keys_1 = kv_rows(1, y, z), kv_rows(0, y, z)
    for c in local[:3]:
        c.wait()
    project_kv(head_b, far_kv)
    send(Y_KVA, far_kv, keys_a, partner)
    project_kv(head_a, keys_a)
    for d in (2, 1, 3):
        send(Z_KVA + d, keys_a, keys_a, at(zs(d), y, x))
    for c in local[3:]:
        c.wait()
    own_1[1] = cot_v[:, HD : 2 * HD]
    own_a[1] = cot_v[:, aligned(head_a, HD)]
    far_qg[1] = cot_v[:, aligned(head_b, HD)]
    v = dot(h_v[...], jnp.concatenate([columns(0, head_b), columns(0, head_a)], axis=1))
    far_qg[0] = v[:, :HD].astype(BF16)
    own_a[0] = v[:, HD:].astype(BF16)
    send(Y_QG, far_qg, own_a, partner)
    for d in (2, 1, 3):
        send(X_QGA + d, own_a, own_a, at(z, y, xs(d)))

    got(Y_KVA, kv_rows(1, other, z))
    for d in (2, 1, 3):
        send(Z_KVAR + d, kv_rows(1, other, z), kv_rows(1, other, z), at(zs(d), y, x))
    project_kv(1, keys_1)
    own_1[0] = dot(h_v[...], columns(0, 1)).astype(BF16)
    got(Y_QG, qg_slot(other, x))
    for d in (2, 1, 3):
        send(X_QGR + d, qg_slot(other, x), qg_slot(other, x), at(z, y, xs(d)))
    sm[...] = jnp.zeros_like(sm)
    ma[...] = jnp.zeros_like(ma)

    def hidden_rows(i, _):
        ht[i] = h_v[:, aligned(i, 384)].T.reshape(NX, 96, T)
        return 0

    lax.fori_loop(0, NZ * NY, hidden_rows, 0)
    hx[x] = ht[:, x]

    def transpose_block(j, yy, zz):
        i = yy * NZ + zz
        vkt[0:HD, aligned(i, T)] = kv[j, 1, aligned(i, T), :].T
        vkt[HD : 2 * HD, aligned(i, T)] = kv[j, 0, aligned(i, T), :].T

    def transpose_keys(j, base, base_relay):
        def step(d, _):
            zz = zs(4 - d)
            if base is not None:

                @pl.when(d != 0)
                def _():
                    got(base + d, kv_rows(j, y, zz))
                    got(base_relay + d, kv_rows(j, other, zz))

            transpose_block(j, y, zz)
            transpose_block(j, other, zz)
            return 0

        lax.fori_loop(0, 4, step, 0)

    transpose_keys(1, Z_KVA, Z_KVAR)

    send(Y_KV1, keys_1, keys_1, partner)
    half = pl.ds(4 * core, 4)
    rows_sent = []
    for d in (2, 1, 3):
        send(Z_KV1 + d, keys_1, keys_1, at(zs(d), y, x))
        rows_sent.append(remote(X_HX + d, ht.at[half, xs(d)], hx.at[x, half], at(z, y, xs(d))))
        rows_sent[-1].start()
    for d in RING:
        send(X_QG1 + d, own_1, own_1, at(z, y, xs(d)))

    chunks = [slice(c * CHUNK, (c + 1) * CHUNK) for c in range(KEYS // CHUNK)]

    def scores(j, q_slot, c, top):
        s = dot(kv[j, 0, c, :], qg[q_slot, 0], NT)
        s_buf[c] = s
        return jnp.maximum(top, jnp.max(s, axis=0, keepdims=True))

    least = jnp.full((1, T), -jnp.inf, F32)

    def unit(j, q_slot, slot, row, following):
        g = qg[q_slot, 1]
        top = top_buf[0:1] * LOG2
        total, out = 0.0, 0.0
        for c in chunks:
            p = jnp.exp2(s_buf[c] * LOG2 - top)
            total = total + jnp.sum(p, axis=0, keepdims=True)
            p = p.astype(BF16)
            pt[slot, c, :] = p
            out = out + dot(vkt[:, c], p)
        g_t = g.astype(F32).T
        delta = jnp.sum(g_t * out[:HD], axis=0, keepdims=True) / total
        grad, top_next = 0.0, least
        for c in chunks:
            if following is not None:
                top_next = scores(*following, c, top_next)
            dp = dot(kv[j, 1, c, :], g, NT)
            d = (pt[slot, c, :].astype(F32) * (dp - delta)).astype(BF16)
            ut[slot, c, :] = d
            grad = grad + dot(vkt[HD:, c], d)
        st[slot, : 2 * HD] = out
        st[slot, 2 * HD :] = grad
        sm[j, 0, pl.ds(row, 1), :] = top + jnp.log2(total)
        sm[j, 1, pl.ds(row, 1), :] = delta
        ma[j, pl.ds(row, 1), :] = top
        top_buf[0:1] = top_next

    def row_a(i):
        yy = (y + i // 4) % 2
        return yy, xs(4 - i % 4), yy * NX + xs(4 - i % 4)

    def relay_shared():
        rows = kv_rows(0, other, z)
        return [remote(Z_KV1R + d, rows, rows, at(zs(d), y, x)) for d in (1, 3)]

    def cross_shared():
        rows = kv_rows(0, y, zs(2))
        return remote(Z_KV1R + 2, rows, rows, partner)

    def unit_a(i, _):
        _, _, r = row_a(i)
        _, _, r_next = row_a(i + 1)

        @pl.when((i != 3) & (i != 7))
        def _():
            got(X_QGA + i + 1, qg.at[4 + r_next])

        @pl.when(i == 3)
        def _():
            got(Y_KV1, kv_rows(0, other, z))
            for c in relay_shared():
                c.start()
            got(Z_KV1 + 2, kv_rows(0, y, zs(2)))
            cross_shared().start()

        @pl.when(i == 7)
        def _():
            for d in (1, 3):
                got(Z_KV1 + d, kv_rows(0, y, zs(4 - d)))
            for d in RING:
                got(Z_KV1R + d, kv_rows(0, other, zs(4 - d)))

        last = i // 7
        unit(1, 4 + r, r, r, (1 - last, jnp.where(last == 1, x, 4 + r_next)))
        return 0

    top = least
    for c in chunks:
        top = scores(1, 4 + y * NX + x, c, top)
    top_buf[0:1] = top
    lax.fori_loop(0, 8, unit_a, 0)
    sent.extend(relay_shared() + [cross_shared()])

    def send_stats(j, base):
        for d in RING:
            send(base + d, sm.at[j], sm_all.at[j, x], at(z, y, xs(d)))
        sm_all[j, x] = sm[j]

    def combine(j, base):
        for d in RING:
            got(base + d, sm_all.at[j, xs(4 - d)])
        lse = sm_all[j, :, 0]
        top = jnp.max(lse, axis=0)
        lse_all = top + jnp.log2(jnp.sum(jnp.exp2(lse - top), axis=0))
        delta = jnp.sum(jnp.exp2(lse - lse_all) * sm_all[j, :, 1], axis=0)
        cs[j] = jnp.exp2(ma[j] - lse_all)
        es[j] = delta - sm[j, 1]

    send_stats(1, X_STA)
    for d in RING:
        part = hx.at[xs(4 - d), half]
        got(X_HX + d, part)
        send(C_HX + d, part, part, (me, mate))
    transpose_keys(0, None, None)
    got(X_QG1 + 1, qg.at[xs(3)])
    unit(0, x, 8, x, (0, xs(3)))
    combine(1, X_STA)

    def prepare(j, row, slot, q_slot, r, b):
        c, e = cs[j, pl.ds(row, 1), :], es[j, pl.ds(row, 1), :]
        o = st[slot, 0:HD] * c
        dq = (st[slot, 2 * HD :] - e * st[slot, HD : 2 * HD]) * (c * SCALE)
        ob[b, 0] = o.T.astype(BF16)
        ob[b, 1] = dq.T.astype(BF16)
        cols = jnp.concatenate([c, e, jnp.zeros((6, T), F32)], axis=0).T
        c, e = cols[:, 0:1], cols[:, 1:2]
        cq = c * qg[q_slot, 0].astype(F32)
        rhs[r, :, 0:HD] = (c * qg[q_slot, 1].astype(F32)).astype(BF16)
        rhs[r, :, HD : 2 * HD] = (e * cq).astype(BF16)
        rhs[r, :, 2 * HD :] = cq.astype(BF16)

    def copy_o(kind, d, b):
        return pltpu.make_async_remote_copy(
            src_ref=ob.at[b], dst_ref=ro.at[kind, x], send_sem=sem_os.at[kind, d], recv_sem=sem_or.at[kind, d],
            device_id=at(z, y, xs(4 - d)), device_id_type=MESH,
        )

    def got_o(kind):
        def step(d):
            dst = ro.at[kind, xs(d)]
            pltpu.make_async_remote_copy(
                src_ref=dst, dst_ref=dst, send_sem=sem_os.at[kind, d], recv_sem=sem_or.at[kind, d],
                device_id=partner, device_id_type=MESH,
            ).wait_recv()

        loop(1, 4, step)

    def send_a(i):
        return copy_o(i // 4, i % 4, row_a(i)[2])

    def loop(first, last, step):
        def body(i, _):
            step(i)
            return 0

        lax.fori_loop(first, last, body, 0)

    def prepare_a(k):
        i = 7 - k
        _, _, r = row_a(i)
        prepare(1, r, r, 4 + r, r, r)

        @pl.when(i % 4 != 0)
        def _():
            send_a(i).start()

    loop(0, 8, prepare_a)
    ro[0, x] = ob[y * NX + x]
    ro[1, x] = ob[other * NX + x]

    def k_block(row, zz):
        return ((y + row) % 2) * NZ + zz

    def k_part(kind):
        return pl.ds(0, 2) if kind < 2 else pl.ds(1, 1) if kind < 4 else pl.ds(0, 1)

    def k_slots(kind):
        return (2 if kind < 2 else 0) + kind % 2

    def copy_k(kind, d):
        src = kb.at[k_block(kind % 2, zs(d)), k_part(kind)]
        return pltpu.make_async_remote_copy(
            src_ref=src, dst_ref=rk.at[k_slots(kind), z, k_part(kind)], send_sem=sem_ks.at[kind, d],
            recv_sem=sem_kr.at[kind, d], device_id=at(zs(d), y, x), device_id_type=MESH,
        )

    def got_k(kind):
        def step(d):
            dst = rk.at[k_slots(kind), zs(4 - d), k_part(kind)]
            pltpu.make_async_remote_copy(
                src_ref=dst, dst_ref=dst, send_sem=sem_ks.at[kind, d],
                recv_sem=sem_kr.at[kind, d], device_id=partner, device_id_type=MESH,
            ).wait_recv()

        loop(1, 4, step)

    def key_blocks(step, kind):
        for row in (1, 0):

            def one(k, row=row):
                zz = 2 * ((z // 2 + 1 + k) % 2)
                b = k_block(row, zz)
                step(b)
                for i in (0, 1):
                    d = (zz + i + NZ - z) % NZ

                    @pl.when(d != 0)
                    def _():
                        copy_k(kind + row, d).start()

            loop(0, 2, one)
            b, part = k_block(row, z), k_part(kind)
            rk[k_slots(kind + row), z, part] = kb[b, part]

    def two_rows(i):
        return pl.ds(pl.multiple_of(i * T, 2 * T), 2 * T)

    def put(b, part, v):
        kb[b, part] = v[:T].astype(BF16)
        kb[b + 1, part] = v[T:].astype(BF16)

    def block_a(i):
        dv = dk = 0.0
        for r in range(8):
            dv = dv + dot(pt[r, two_rows(i), :], rhs[r, :, : 2 * HD])
            dk = dk + dot(ut[r, two_rows(i), :], rhs[r, :, 2 * HD :])
        put(i, 0, (dk - dv[:, HD:]) * SCALE)
        put(i, 1, dv[:, :HD])

    shared_slots = (8, 0, 1, 2)

    def block_v(i):
        dv = 0.0
        for r, slot in enumerate(shared_slots):
            dv = dv + dot(pt[slot, two_rows(i), :], rhs[r, :, : 2 * HD])
        st[i, : 2 * HD, :HD] = dv[:T, HD:]
        st[i + 1, : 2 * HD, :HD] = dv[T:, HD:]
        put(i, 1, dv[:, :HD])

    def block_k(i):
        dk = 0.0
        for r, slot in enumerate(shared_slots):
            dk = dk + dot(ut[slot, two_rows(i), :], rhs[r, :, 2 * HD :])
        put(i, 0, (dk - jnp.concatenate([st[i, : 2 * HD, :HD], st[i + 1, : 2 * HD, :HD]], axis=0)) * SCALE)

    key_blocks(block_a, 0)

    def total(ref, kind, part):
        v = ref[kind, 0, part].astype(F32)
        for i in range(1, 4):
            v = v + ref[kind, i, part].astype(F32)
        return v

    mine, theirs = aligned(y, HD), aligned(other, HD)
    q_part, kv_part = pl.ds(0, 1), pl.ds(1, 2)

    def piece_a(d, part, cols):
        return gx_a.at[xs(d), part, :, cols]

    def gather_a(base, part, cols):
        piece = piece_a(0, part, cols)
        return [remote(base + d, piece, piece, at(z, y, xs(d))) for d in (1, 3)]

    def pass_on(base, part, cols, step):
        piece = piece_a(4 - step, part, cols)
        return remote(base + 2, piece, piece, at(z, y, xs(step)))

    def forward_a(base, part, cols, step):
        got(base + step, piece_a(4 - step, part, cols))
        pass_on(base, part, cols, step).start()

    pieces = {X_GA: (q_part, mine, 1), X_GB: (q_part, theirs, 3), X_GC: (kv_part, mine, 1), X_GD: (kv_part, theirs, 3)}

    def got_a(base):
        part, cols, step = pieces[base]
        got(base + 4 - step, piece_a(step, part, cols))
        got(base + 2, piece_a(2, part, cols))

    def far_o():
        return remote(Y_OA, ya_s.at[pl.ds(0, 2)], ya_r.at[pl.ds(0, 2)], partner)

    def far_k():
        return remote(Y_KA, ya_s.at[pl.ds(2, 2)], ya_r.at[pl.ds(2, 2)], partner)

    def start_all(copies):
        for c in copies:
            c.start()

    def unit_shared(d):
        got(X_QG1 + d + 1, qg.at[xs(3 - d)])
        unit(0, xs(4 - d), d - 1, xs(4 - d), (0, xs(3 - d)))

        @pl.when(d == 1)
        def _():
            got_o(1)
            for part in (0, 1):
                ya_s[part] = total(ro, 1, part).astype(BF16)
            far_o().start()
            got_o(0)
            att_ref[:, aligned(head_a, HD)] = total(ro, 0, 0).astype(BF16)
            gx_a[x, 0, :, mine] = total(ro, 0, 1).astype(BF16)
            start_all(gather_a(X_GA, q_part, mine))

        @pl.when(d == 2)
        def _():
            got_k(1)
            for part in (0, 1):
                ya_s[2 + part] = total(rk, 3, part).astype(BF16)
            far_k().start()
            got(Y_OA, ya_r.at[pl.ds(0, 2)])
            att_ref[:, aligned(head_b, HD)] = ya_r[0]
            gx_a[x, 0, :, theirs] = ya_r[1]
            start_all(gather_a(X_GB, q_part, theirs))
            got_k(0)
            for part in (0, 1):
                gx_a[x, 1 + part, :, mine] = total(rk, 2, part).astype(BF16)
            start_all(gather_a(X_GC, kv_part, mine))
            forward_a(X_GA, q_part, mine, 1)

    loop(1, 3, unit_shared)
    unit(0, xs(1), 2, xs(1), None)
    send_stats(0, X_ST1)
    got(Y_KA, ya_r.at[pl.ds(2, 2)])
    for c in (1, 2):
        gx_a[x, c, :, theirs] = ya_r[1 + c]
    start_all(gather_a(X_GD, kv_part, theirs))
    sent.extend([far_o(), far_k()])
    forward_a(X_GB, q_part, theirs, 3)
    for base, (part, cols, step) in pieces.items():
        sent.extend(gather_a(base, part, cols))
        sent.append(pass_on(base, part, cols, step))

    combine(0, X_ST1)

    def send_shared(d):
        return copy_o(2, d, xs(4 - d))

    def prepare_shared(d):
        slot = (d + 8) % 9
        prepare(0, xs(4 - d), slot, xs(4 - d), d, xs(4 - d))

        @pl.when(d != 0)
        def _():
            send_shared(d).start()

    for c in range(2):
        loop(1, 4, lambda d, c=c: send_a(4 * c + d).wait_send())
    loop(0, 4, prepare_shared)
    ro[2, x] = ob[x]

    forward_a(X_GC, kv_part, mine, 1)
    for kind in (0, 1):
        loop(1, 4, lambda d, kind=kind: copy_k(kind, d).wait_send())
    key_blocks(block_v, 2)
    forward_a(X_GD, kv_part, theirs, 3)
    key_blocks(block_k, 4)

    def copy_w(c, d):
        ref, dst = (dwb_h, dwr_h) if c >= 3 else (dwb_a, dwr_a)
        return pltpu.make_async_remote_copy(
            src_ref=ref.at[zs(d), c % 3], dst_ref=dst.at[z, c % 3], send_sem=sem_ws.at[c, d],
            recv_sem=sem_wr.at[c, d], device_id=at(zs(d), y, x), device_id_type=MESH,
        )

    def got_w(c):
        def step(d):
            dst = (dwr_h if c >= 3 else dwr_a).at[zs(4 - d), c % 3]
            pltpu.make_async_remote_copy(
                src_ref=dst, dst_ref=dst, send_sem=sem_ws.at[c, d], recv_sem=sem_wr.at[c, d],
                device_id=partner, device_id_type=MESH,
            ).wait_recv()

        loop(1, 4, step)

    def weight_rows(c):
        gx, dwb, dwr = (gx_h, dwb_h, dwr_h) if c >= 3 else (gx_a, dwb_a, dwr_a)

        def step(i):
            v = 0.0
            for xx in range(NX):
                v = v + dot(hx[xx, pl.ds(i * 4, 4)].reshape(4 * 96, T), gx[xx, c % 3])
            dwb[pl.ds(i * 2, 2), c % 3] = v.astype(BF16).reshape(2, 2, 96, v.shape[1])

        loop(0, 2, step)
        loop(1, 4, lambda d: copy_w(c, d).start())
        dwr[z, c % 3] = dwb[z, c % 3]

    got_o(2)
    att_ref[:, HD : 2 * HD] = total(ro, 2, 0).astype(BF16)
    gx_h[x, 0] = total(ro, 2, 1).astype(BF16)
    for d in RING:
        send(X_GHQ + d, gx_h.at[x, 0], gx_h.at[x, 0], at(z, y, xs(d)))
    got_k(3)
    y1_s[1] = total(rk, 1, 1).astype(BF16)
    send(Y_V1, y1_s.at[1], y1_r.at[1], partner)

    for d in RING:
        got(C_HX + d, hx.at[xs(4 - d), pl.ds(4 - 4 * core, 4)])
    got_a(X_GA)
    got_a(X_GB)
    weight_rows(0)

    got_k(2)
    got(Y_V1, y1_r.at[1])
    gx_h[x, 2] = (total(rk, 0, 1) + y1_r[1].astype(F32)).astype(BF16)
    for d in RING:
        send(X_GHV + d, gx_h.at[x, 2], gx_h.at[x, 2], at(z, y, xs(d)))
    got_a(X_GC)
    got_a(X_GD)
    weight_rows(1)
    got_k(5)
    y1_s[0] = total(rk, 1, 0).astype(BF16)
    send(Y_K1, y1_s.at[0], y1_r.at[0], partner)
    weight_rows(2)
    got_k(4)
    got(Y_K1, y1_r.at[0])
    gx_h[x, 1] = (total(rk, 0, 0) + y1_r[0].astype(F32)).astype(BF16)
    for d in RING:
        send(X_GHK + d, gx_h.at[x, 1], gx_h.at[x, 1], at(z, y, xs(d)))

    for c in rows_sent:
        c.wait_send()

    def part_of(to):
        return ht.at[pl.ds(2 * to, 2)]

    def hidden_part(to):
        pieces = []
        for i in range(3):
            v = 0.0
            for c in range(3):
                g = jnp.concatenate([gx_a[x, c, :, :HD], gx_h[x, c], gx_a[x, c, :, HD:]], axis=1)
                rows = pl.ds(pl.multiple_of(to * 768 + i * 256, 256), 256)
                v = v + dot(g, w_v[c, rows, :], NT)
            pieces.append(v.astype(BF16))
        part_of(to)[...] = jnp.concatenate(pieces, axis=0).reshape(2, NX, 96, T)

    def hidden_mate(i):
        hidden_part(2 * i + 1 - core)
        copy_mate(i).start()

    def copy_mate(i):
        return remote(C_DH + i, part_of(2 * i + 1 - core), dhc.at[i], (me, mate))

    loop(0, 2, hidden_mate)
    loop(0, 2, lambda i: hidden_part(2 * i + core))
    for i in range(2):
        sent.append(copy_mate(i))
        got(C_DH + i, dhc.at[i])
    hi = t // 2
    far = part_of(across)
    far[...] = (far[...].astype(F32) + dhc[1 - hi].astype(F32)).astype(BF16)
    send(H_DH, far, dhr, (me, across))

    for c, base in ((0, X_GHQ), (2, X_GHV), (1, X_GHK)):
        for d in RING:
            got(base + d, gx_h.at[xs(4 - d), c])
        weight_rows(3 + c)

    def total_w(ref, c, row):
        v = ref[0, c, row].astype(F32)
        for i in range(1, NZ):
            v = v + ref[i, c, row].astype(F32)
        return v

    for c in range(3):
        got_w(c)
        ywa_s[c] = total_w(dwr_a, c, other).astype(BF16)
    send(Y_WA, ywa_s, ywa_r, partner)
    for c in range(3):
        got_w(3 + c)
        yw1_s[c] = total_w(dwr_h, c, other).astype(BF16)
    send(Y_W1, yw1_s, yw1_r, partner)
    got(Y_WA, ywa_r)
    for c in range(3):
        v = total_w(dwr_a, c, y) + ywa_r[c].astype(F32)
        dw_ref[c, :, :HD] = v[:, :HD]
        dw_ref[c, :, 2 * HD :] = v[:, HD:]
    got(Y_W1, yw1_r)
    for c in range(3):
        dw_ref[c, :, HD : 2 * HD] = total_w(dwr_h, c, y) + yw1_r[c].astype(F32)
    got(H_DH, dhr)
    v = (part_of(t)[...].astype(F32) + dhc[hi].astype(F32) + dhr[...].astype(F32)).astype(BF16).reshape(3 * T, T)
    for i in range(3):
        dh_ref[:, i * T : (i + 1) * T] = v[i * T : (i + 1) * T]

    for c in sent:
        c.wait_send()
    loop(1, 4, lambda d: send_shared(d).wait_send())
    for kind in range(6):
        if kind > 1:
            loop(1, 4, lambda d, kind=kind: copy_k(kind, d).wait_send())
        loop(1, 4, lambda d, c=kind: copy_w(c, d).wait_send())


def call(hidden, weight, cotangent):
    block = (2, T, HD)
    scratch = [
        ((T, 3072), BF16),
        ((3, 3072, 384), BF16),
        ((T, 3 * HD), BF16),
        (block, BF16),
        (block, BF16),
        ((8, NX, 96, T), BF16),
        ((NX, 8, 96, T), BF16),
        ((12,) + block, BF16),
        ((2, 2, KEYS, HD), BF16),
        ((2 * HD, KEYS), BF16),
        ((9, KEYS, T), BF16),
        ((9, KEYS, T), BF16),
        ((KEYS, T), F32),
        ((8, T), F32),
        ((9, 3 * HD, T), F32),
        ((2, 2, 8, T), F32),
        ((2, NX, 2, 8, T), F32),
        ((2, 8, T), F32),
        ((2, 8, T), F32),
        ((2, 8, T), F32),
        ((8, T, 3 * HD), BF16),
        ((8,) + block, BF16),
        ((3, NX) + block, BF16),
        ((8,) + block, BF16),
        ((4, NZ) + block, BF16),
        ((4, T, HD), BF16),
        ((4, T, HD), BF16),
        (block, BF16),
        (block, BF16),
        ((3, 96, 2 * HD), BF16),
        ((3, 96, 2 * HD), BF16),
        ((3, 96, HD), BF16),
        ((3, 96, HD), BF16),
        ((NX, 3, T, 2 * HD), BF16),
        ((NX, 3, T, HD), BF16),
        ((NZ, 3, 2, 96, 2 * HD), BF16),
        ((NZ, 3, 2, 96, 2 * HD), BF16),
        ((NZ, 3, 2, 96, HD), BF16),
        ((NZ, 3, 2, 96, HD), BF16),
        ((2, 2, NX, 96, T), BF16),
        ((2, NX, 96, T), BF16),
    ]
    sems = [(5,), (N_SEM,), (N_SEM,), (3, 4), (3, 4), (6, 4), (6, 4), (6, 4), (6, 4)]
    vmem = pl.BlockSpec(memory_space=pltpu.VMEM)
    hbm = pl.BlockSpec(memory_space=pl.ANY)
    return pl.pallas_call(
        kernel,
        out_shape=(
            jax.ShapeDtypeStruct((T, 3 * HD), BF16),
            jax.ShapeDtypeStruct((3, 96, 384), F32),
            jax.ShapeDtypeStruct((T, 768), BF16),
        ),
        in_specs=[hbm] * 3,
        out_specs=(vmem,) * 3,
        scratch_shapes=[pltpu.VMEM(*s) for s in scratch] + [pltpu.SemaphoreType.DMA(s) for s in sems],
        compiler_params=pltpu.CompilerParams(
            collective_id=0, has_side_effects=True, vmem_limit_bytes=63 * 2**20
        ),
        cost_estimate=pl.CostEstimate(flops=18 * 10**9, bytes_accessed=10**7, transcendentals=6 * 10**6),
        name="attention_with_gradients",
    )(hidden, weight, cotangent)


def copy_kernel(*refs):
    for src, dst in zip(refs[:3], refs[3:]):
        dst[...] = src[...]


def copy_out(arrays):
    vmem = pl.BlockSpec(memory_space=pltpu.VMEM)
    return pl.pallas_call(
        copy_kernel,
        out_shape=tuple(jax.ShapeDtypeStruct(a.shape, a.dtype) for a in arrays),
        in_specs=[vmem] * 3,
        out_specs=(vmem,) * 3,
        name="copy_out",
    )(*arrays)


def on_device(hidden, qkv_weight, cotangent):
    arrays = call(hidden, qkv_weight.transpose(1, 0, 2), cotangent)
    attention, grad_weight, grad_hidden = copy_out(arrays)
    return attention, grad_hidden, grad_weight.transpose(1, 0, 2)


def solution(mesh):
    in_specs = (P("seq", None), P(None, None, "tp"), P("seq", "tp"))
    out_specs = (P("seq", "tp"), P("seq", "tp"), P("seq", None, "tp"))
    return jax.shard_map(
        on_device, mesh=mesh, in_specs=in_specs, out_specs=out_specs, check_vma=False
    )
```

time: 118 us -> 107 us (0.907)
  Pallas kernels: 112 us -> 105 us
  local copies, waits for them, and re-layouts: 5.19 us -> 0 us
    pallas_call x1, Pallas kernels: 112 us -> 103 us  [call(): pl.pallas_call(kernel, out_shape=(jax.ShapeDtypeStruct((T, 3 * HD), BF16)...]
    unnamed x3 -> x0, local copies, waits for them, and re-layouts: 5.19 us -> none
    pallas_call x0 -> x1, Pallas kernels: none -> 2.21 us  [copy_out(): pl.pallas_call(copy_kernel, out_shape=tuple((jax.ShapeDtypeStruct(a.shape...]
where the time goes in v3:
time: 107 us; the launch traced here: 106 us
  Pallas kernels  105 us (98%)
    pallas_call x1, Pallas kernels, call(): pl.pallas_call(kernel, out_shape=(jax.ShapeDtypeStruct((T, 3 * HD), BF16)...  103 us
    pallas_call x1, Pallas kernels, copy_out(): pl.pallas_call(copy_kernel, out_shape=tuple((jax.ShapeDtypeStruct(a.shape...  2.21 us

profile of v3, /device:TPU:16, one launch (start us, length us, event | category | flops | bytes accessed | tf_op | source)
XLA Modules:
  0.0 105.8 jit_solution(2588464990020663138)
XLA Ops:
  0.6 103.0 %attention_with_gradients.1 = (bf16[256,384]{1,0:T(8,128)(2,1)}, f32[3,96,384]{2,1,0:T(8,128)}, bf16[256,768]{1,0:T(8,128)(2,1)}) custom-call(bf16[256,3072]{1,0:T(8,128)(2,1)} %hidden_ref.1, bf16[3,3072,384]{2,1,0:T(8,128)(2,1)} %bitcast.2, bf16[256,384]{1,0:T(8,128)(2,1)} %cot_ref.1), custom_call_target="tpu_custom_call" | custom-call | flops 17999998976 | bytes 10000000 | tf_op jit(solution)/shard_map/attention_with_gradients/pallas_call | solution.py:725
  103.6 2.2 %copy_out.1 = (bf16[256,384]{1,0:T(8,128)(2,1)}, f32[3,96,384]{2,1,0:T(8,128)}, bf16[256,768]{1,0:T(8,128)(2,1)}) custom-call(bf16[256,384]{1,0:T(8,128)(2,1)} %get-tuple-element.9.refs_0_, f32[3,96,384]{2,1,0:T(8,128)} %get-tuple-element.10.refs_1_, bf16[256,768]{1,0:T(8,128)(2,1)} %get-tuple-element.11.refs_2_), custom_call_target="tpu_custom_call" | custom-call | tf_op jit(solution)/shard_map/copy_out/pallas_call | solution.py:750

commit v4 on v3

--- a/solution.py
+++ b/solution.py
@@ -42,9 +42,10 @@
 X_HX, C_HX, X_STA, X_ST1 = 31, 35, 39, 43
 X_GA, X_GHV, X_GHK, X_GHQ = 47, 51, 55, 67
 C_DH, H_DH = 59, 61
-Y_OA, Y_KA, Y_V1, Y_K1, Y_WA, Y_W1 = 62, 63, 64, 65, 66, 67
-X_GB, X_GC, X_GD, N_SEM = 71, 75, 79, 83
+Y_OA, Y_KA, Y_V1, Y_K1, Y_W1, Y_WA = 62, 63, 64, 65, 66, 83
+X_GB, X_GC, X_GD, N_SEM = 71, 75, 79, 86
 RING = (1, 2, 3)
+CROSS_FIRST = (0,)
 
 
 def kernel(
@@ -71,13 +72,16 @@
     def zs(d):
         return (z + d) % NZ
 
-    local = [
-        pltpu.make_async_copy(hidden_ref, h_v, sem_l.at[0]),
-        pltpu.make_async_copy(w_ref.at[1], w_v.at[1], sem_l.at[1]),
-        pltpu.make_async_copy(w_ref.at[2], w_v.at[2], sem_l.at[2]),
-        pltpu.make_async_copy(w_ref.at[0], w_v.at[0], sem_l.at[3]),
-        pltpu.make_async_copy(cot_ref, cot_v, sem_l.at[4]),
-    ]
+    def load(i, src, dst):
+        return pltpu.make_async_copy(src, dst, sem_l.at[i])
+
+    def load_w(i, c, h):
+        cols = aligned(h, HD)
+        return load(i, w_ref.at[c, :, cols], w_v.at[c, :, cols])
+
+    local = [load(0, hidden_ref, h_v), load_w(1, 1, head_b), load_w(2, 2, head_b), load_w(3, 1, head_a), load_w(4, 2, head_a)]
+    local += [load_w(5, 0, head_b), load_w(6, 0, head_a), load(7, cot_ref, cot_v)]
+    local += [load_w(8 + c, c, 1) for c in range(3)]
     for c in local:
         c.start()
 
@@ -124,10 +128,12 @@
         c.wait()
     project_kv(head_b, far_kv)
     send(Y_KVA, far_kv, keys_a, partner)
+    for c in local[3:5]:
+        c.wait()
     project_kv(head_a, keys_a)
-    for d in (2, 1, 3):
+    for d in (1, 3):
         send(Z_KVA + d, keys_a, keys_a, at(zs(d), y, x))
-    for c in local[3:]:
+    for c in local[5:8]:
         c.wait()
     own_1[1] = cot_v[:, HD : 2 * HD]
     own_a[1] = cot_v[:, aligned(head_a, HD)]
@@ -136,17 +142,34 @@
     far_qg[0] = v[:, :HD].astype(BF16)
     own_a[0] = v[:, HD:].astype(BF16)
     send(Y_QG, far_qg, own_a, partner)
-    for d in (2, 1, 3):
+    for d in (1, 3):
         send(X_QGA + d, own_a, own_a, at(z, y, xs(d)))
 
     got(Y_KVA, kv_rows(1, other, z))
-    for d in (2, 1, 3):
+    for d in (1, 3):
         send(Z_KVAR + d, kv_rows(1, other, z), kv_rows(1, other, z), at(zs(d), y, x))
+
+    def forward_keys(base, yy):
+        for part, step in ((0, 1), (1, 3)):
+            got(base + step, kv_rows(1, yy, zs(4 - step)))
+            piece = kv.at[1, part, aligned(yy * NZ + zs(4 - step), T), :]
+            send(base + 2 - 2 * part, piece, piece, at(zs(step), y, x))
+
+    def forward_queries(base, yy):
+        for part, step in ((0, 1), (1, 3)):
+            got(base + step, qg_slot(yy, xs(4 - step)))
+            piece = qg.at[4 + yy * NX + xs(4 - step), part]
+            send(base + 2 - 2 * part, piece, piece, at(z, y, xs(step)))
+
+    forward_keys(Z_KVA, y)
+    for c in local[8:]:
+        c.wait()
     project_kv(1, keys_1)
     own_1[0] = dot(h_v[...], columns(0, 1)).astype(BF16)
     got(Y_QG, qg_slot(other, x))
-    for d in (2, 1, 3):
+    for d in (1, 3):
         send(X_QGR + d, qg_slot(other, x), qg_slot(other, x), at(z, y, xs(d)))
+    forward_queries(X_QGA, y)
     sm[...] = jnp.zeros_like(sm)
     ma[...] = jnp.zeros_like(ma)
 
@@ -167,17 +190,20 @@
             zz = zs(4 - d)
             if base is not None:
 
-                @pl.when(d != 0)
+                @pl.when(d == 2)
                 def _():
-                    got(base + d, kv_rows(j, y, zz))
-                    got(base_relay + d, kv_rows(j, other, zz))
+                    for part in (0, 1):
+                        got(base + 2 - 2 * part, kv.at[j, part, aligned(y * NZ + zz, T), :])
+                        got(base_relay + 2 - 2 * part, kv.at[j, part, aligned(other * NZ + zz, T), :])
 
             transpose_block(j, y, zz)
             transpose_block(j, other, zz)
             return 0
 
-        lax.fori_loop(0, 4, step, 0)
-
+        lax.fori_loop(3, 7, lambda d, _: step(d % 4, _), 0)
+
+    forward_keys(Z_KVAR, other)
+    forward_queries(X_QGR, other)
     transpose_keys(1, Z_KVA, Z_KVAR)
 
     send(Y_KV1, keys_1, keys_1, partner)
@@ -242,9 +268,10 @@
         _, _, r = row_a(i)
         _, _, r_next = row_a(i + 1)
 
-        @pl.when((i != 3) & (i != 7))
+        @pl.when((i == 1) | (i == 5))
         def _():
-            got(X_QGA + i + 1, qg.at[4 + r_next])
+            for part in (0, 1):
+                got(X_QGA + i + 1 - 2 * part, qg.at[4 + r_next, part])
 
         @pl.when(i == 3)
         def _():
@@ -511,6 +538,57 @@
         sent.extend(gather_a(base, part, cols))
         sent.append(pass_on(base, part, cols, step))
 
+    def copy_w(c, d):
+        if c in CROSS_FIRST:
+            src, dst = dwb_a.at[zs(d), c, y], dwr_a.at[z, c, y]
+        elif c < 3:
+            src, dst = dwb_a.at[zs(d), c], dwr_a.at[z, c]
+        else:
+            src, dst = dwb_h.at[zs(d), c - 3], dwr_h.at[z, c - 3]
+        return pltpu.make_async_remote_copy(
+            src_ref=src, dst_ref=dst, send_sem=sem_ws.at[c, d],
+            recv_sem=sem_wr.at[c, d], device_id=at(zs(d), y, x), device_id_type=MESH,
+        )
+
+    def got_w(c):
+        def step(d):
+            dst = (dwr_h if c >= 3 else dwr_a).at[zs(4 - d), c % 3]
+            dst = dst.at[y] if c in CROSS_FIRST else dst
+            pltpu.make_async_remote_copy(
+                src_ref=dst, dst_ref=dst, send_sem=sem_ws.at[c, d], recv_sem=sem_wr.at[c, d],
+                device_id=partner, device_id_type=MESH,
+            ).wait_recv()
+
+        loop(1, 4, step)
+
+    def weight_rows(gx, dwb, c):
+        def step(i):
+            v = 0.0
+            for xx in range(NX):
+                v = v + dot(hx[xx, pl.ds(i * 4, 4)].reshape(4 * 96, T), gx[xx, c])
+            dwb[pl.ds(i * 2, 2), c] = v.astype(BF16).reshape(2, 2, 96, v.shape[1])
+
+        loop(0, 2, step)
+
+    def weight_a(c):
+        weight_rows(gx_a, dwb_a, c)
+        if c in CROSS_FIRST:
+            send(Y_WA + c, dwb_a.at[:, c, other], ywa_r.at[c], partner)
+        else:
+            loop(1, 4, lambda d: copy_w(c, d).start())
+            dwr_a[z, c] = dwb_a[z, c]
+
+    def weight_a_ring(c):
+        got(Y_WA + c, ywa_r.at[c])
+        dwb_a[:, c, y] = (dwb_a[:, c, y].astype(F32) + ywa_r[c].astype(F32)).astype(BF16)
+        loop(1, 4, lambda d: copy_w(c, d).start())
+        dwr_a[z, c, y] = dwb_a[z, c, y]
+
+    def weight_shared(c):
+        weight_rows(gx_h, dwb_h, c)
+        loop(1, 4, lambda d: copy_w(3 + c, d).start())
+        dwr_h[z, c] = dwb_h[z, c]
+
     combine(0, X_ST1)
 
     def send_shared(d):
@@ -536,68 +614,44 @@
     forward_a(X_GD, kv_part, theirs, 3)
     key_blocks(block_k, 4)
 
-    def copy_w(c, d):
-        ref, dst = (dwb_h, dwr_h) if c >= 3 else (dwb_a, dwr_a)
-        return pltpu.make_async_remote_copy(
-            src_ref=ref.at[zs(d), c % 3], dst_ref=dst.at[z, c % 3], send_sem=sem_ws.at[c, d],
-            recv_sem=sem_wr.at[c, d], device_id=at(zs(d), y, x), device_id_type=MESH,
-        )
-
-    def got_w(c):
-        def step(d):
-            dst = (dwr_h if c >= 3 else dwr_a).at[zs(4 - d), c % 3]
-            pltpu.make_async_remote_copy(
-                src_ref=dst, dst_ref=dst, send_sem=sem_ws.at[c, d], recv_sem=sem_wr.at[c, d],
-                device_id=partner, device_id_type=MESH,
-            ).wait_recv()
-
-        loop(1, 4, step)
-
-    def weight_rows(c):
-        gx, dwb, dwr = (gx_h, dwb_h, dwr_h) if c >= 3 else (gx_a, dwb_a, dwr_a)
-
-        def step(i):
-            v = 0.0
-            for xx in range(NX):
-                v = v + dot(hx[xx, pl.ds(i * 4, 4)].reshape(4 * 96, T), gx[xx, c % 3])
-            dwb[pl.ds(i * 2, 2), c % 3] = v.astype(BF16).reshape(2, 2, 96, v.shape[1])
-
-        loop(0, 2, step)
-        loop(1, 4, lambda d: copy_w(c, d).start())
-        dwr[z, c % 3] = dwb[z, c % 3]
-
-    got_o(2)
-    att_ref[:, HD : 2 * HD] = total(ro, 2, 0).astype(BF16)
-    gx_h[x, 0] = total(ro, 2, 1).astype(BF16)
-    for d in RING:
-        send(X_GHQ + d, gx_h.at[x, 0], gx_h.at[x, 0], at(z, y, xs(d)))
-    got_k(3)
-    y1_s[1] = total(rk, 1, 1).astype(BF16)
-    send(Y_V1, y1_s.at[1], y1_r.at[1], partner)
-
     for d in RING:
         got(C_HX + d, hx.at[xs(4 - d), pl.ds(4 - 4 * core, 4)])
     got_a(X_GA)
     got_a(X_GB)
-    weight_rows(0)
-
+    weight_a(0)
+
+    got_o(2)
+    att_ref[:, HD : 2 * HD] = total(ro, 2, 0).astype(BF16)
+    gx_h[x, 0] = total(ro, 2, 1).astype(BF16)
+
+    def gather_shared(base, c):
+        for d in RING:
+            send(base + d, gx_h.at[x, c], gx_h.at[x, c], at(z, y, xs(d)))
+
+    def got_shared(base, c):
+        for d in RING:
+            got(base + d, gx_h.at[xs(4 - d), c])
+
+    gather_shared(X_GHQ, 0)
+    got_k(3)
+    y1_s[1] = total(rk, 1, 1).astype(BF16)
+    send(Y_V1, y1_s.at[1], y1_r.at[1], partner)
+    weight_a_ring(0)
+    got_a(X_GC)
+    got_a(X_GD)
+    weight_a(2)
     got_k(2)
     got(Y_V1, y1_r.at[1])
     gx_h[x, 2] = (total(rk, 0, 1) + y1_r[1].astype(F32)).astype(BF16)
-    for d in RING:
-        send(X_GHV + d, gx_h.at[x, 2], gx_h.at[x, 2], at(z, y, xs(d)))
-    got_a(X_GC)
-    got_a(X_GD)
-    weight_rows(1)
+    gather_shared(X_GHV, 2)
     got_k(5)
     y1_s[0] = total(rk, 1, 0).astype(BF16)
     send(Y_K1, y1_s.at[0], y1_r.at[0], partner)
-    weight_rows(2)
+    weight_a(1)
     got_k(4)
     got(Y_K1, y1_r.at[0])
     gx_h[x, 1] = (total(rk, 0, 0) + y1_r[0].astype(F32)).astype(BF16)
-    for d in RING:
-        send(X_GHK + d, gx_h.at[x, 1], gx_h.at[x, 1], at(z, y, xs(d)))
+    gather_shared(X_GHK, 1)
 
     for c in rows_sent:
         c.wait_send()
@@ -616,27 +670,28 @@
             pieces.append(v.astype(BF16))
         part_of(to)[...] = jnp.concatenate(pieces, axis=0).reshape(2, NX, 96, T)
 
-    def hidden_mate(i):
+    def copy_mate(i):
+        return remote(C_DH + i, part_of(2 * i + 1 - core), dhc.at[i], (me, mate))
+
+    def hidden_pair(i):
         hidden_part(2 * i + 1 - core)
         copy_mate(i).start()
-
-    def copy_mate(i):
-        return remote(C_DH + i, part_of(2 * i + 1 - core), dhc.at[i], (me, mate))
-
-    loop(0, 2, hidden_mate)
-    loop(0, 2, lambda i: hidden_part(2 * i + core))
-    for i in range(2):
-        sent.append(copy_mate(i))
-        got(C_DH + i, dhc.at[i])
+        hidden_part(2 * i + core)
+
     hi = t // 2
+    hidden_pair(1 - hi)
+    got(C_DH + 1 - hi, dhc.at[1 - hi])
     far = part_of(across)
     far[...] = (far[...].astype(F32) + dhc[1 - hi].astype(F32)).astype(BF16)
     send(H_DH, far, dhr, (me, across))
-
-    for c, base in ((0, X_GHQ), (2, X_GHV), (1, X_GHK)):
-        for d in RING:
-            got(base + d, gx_h.at[xs(4 - d), c])
-        weight_rows(3 + c)
+    got_shared(X_GHQ, 0)
+    weight_shared(0)
+    got_shared(X_GHV, 2)
+    weight_shared(2)
+    got_shared(X_GHK, 1)
+    weight_shared(1)
+    hidden_pair(hi)
+    sent.extend([copy_mate(0), copy_mate(1)])
 
     def total_w(ref, c, row):
         v = ref[0, c, row].astype(F32)
@@ -644,22 +699,28 @@
             v = v + ref[i, c, row].astype(F32)
         return v
 
-    for c in range(3):
+    ring_first = [c for c in range(3) if c not in CROSS_FIRST]
+    for c in ring_first:
         got_w(c)
         ywa_s[c] = total_w(dwr_a, c, other).astype(BF16)
-    send(Y_WA, ywa_s, ywa_r, partner)
+        send(Y_WA + c, ywa_s.at[c], ywa_r.at[c, 0], partner)
     for c in range(3):
         got_w(3 + c)
         yw1_s[c] = total_w(dwr_h, c, other).astype(BF16)
     send(Y_W1, yw1_s, yw1_r, partner)
-    got(Y_WA, ywa_r)
     for c in range(3):
-        v = total_w(dwr_a, c, y) + ywa_r[c].astype(F32)
+        if c in CROSS_FIRST:
+            got_w(c)
+        v = total_w(dwr_a, c, y)
+        if c in ring_first:
+            got(Y_WA + c, ywa_r.at[c, 0])
+            v = v + ywa_r[c, 0].astype(F32)
         dw_ref[c, :, :HD] = v[:, :HD]
         dw_ref[c, :, 2 * HD :] = v[:, HD:]
     got(Y_W1, yw1_r)
     for c in range(3):
         dw_ref[c, :, HD : 2 * HD] = total_w(dwr_h, c, y) + yw1_r[c].astype(F32)
+    got(C_DH + hi, dhc.at[hi])
     got(H_DH, dhr)
     v = (part_of(t)[...].astype(F32) + dhc[hi].astype(F32) + dhr[...].astype(F32)).astype(BF16).reshape(3 * T, T)
     for i in range(3):
@@ -707,7 +768,7 @@
         (block, BF16),
         (block, BF16),
         ((3, 96, 2 * HD), BF16),
-        ((3, 96, 2 * HD), BF16),
+        ((3, NZ, 96, 2 * HD), BF16),
         ((3, 96, HD), BF16),
         ((3, 96, HD), BF16),
         ((NX, 3, T, 2 * HD), BF16),
@@ -719,7 +780,7 @@
         ((2, 2, NX, 96, T), BF16),
         ((2, NX, 96, T), BF16),
     ]
-    sems = [(5,), (N_SEM,), (N_SEM,), (3, 4), (3, 4), (6, 4), (6, 4), (6, 4), (6, 4)]
+    sems = [(11,), (N_SEM,), (N_SEM,), (3, 4), (3, 4), (6, 4), (6, 4), (6, 4), (6, 4)]
     vmem = pl.BlockSpec(memory_space=pltpu.VMEM)
     hbm = pl.BlockSpec(memory_space=pl.ANY)
     return pl.pallas_call(

time: 107 us -> 103 us (0.963); the launches traced: 106 us -> 103 us
  Pallas kernels: 105 us -> 102 us
    pallas_call x1, Pallas kernels: 103 us -> 100 us  [call(): pl.pallas_call(kernel, out_shape=(jax.ShapeDtypeStruct((T, 3 * HD), BF16)...]
where the time goes in v4:
time: 103 us
  Pallas kernels  102 us (99%)
    pallas_call x1, Pallas kernels, call(): pl.pallas_call(kernel, out_shape=(jax.ShapeDtypeStruct((T, 3 * HD), BF16)...  100 us
    pallas_call x1, Pallas kernels, copy_out(): pl.pallas_call(copy_kernel, out_shape=tuple((jax.ShapeDtypeStruct(a.shape...  2.21 us

profile of v4, /device:TPU:16, one launch (start us, length us, event | category | flops | bytes accessed | tf_op | source)
XLA Modules:
  0.0 102.9 jit_solution(214820223608479183)
XLA Ops:
  0.6 100.1 %attention_with_gradients.1 = (bf16[256,384]{1,0:T(8,128)(2,1)}, f32[3,96,384]{2,1,0:T(8,128)}, bf16[256,768]{1,0:T(8,128)(2,1)}) custom-call(bf16[256,3072]{1,0:T(8,128)(2,1)} %hidden_ref.1, bf16[3,3072,384]{2,1,0:T(8,128)(2,1)} %bitcast.2, bf16[256,384]{1,0:T(8,128)(2,1)} %cot_ref.1), custom_call_target="tpu_custom_call" | custom-call | flops 17999998976 | bytes 10000000 | tf_op jit(solution)/shard_map/attention_with_gradients/pallas_call | solution.py:786
  100.7 2.2 %copy_out.1 = (bf16[256,384]{1,0:T(8,128)(2,1)}, f32[3,96,384]{2,1,0:T(8,128)}, bf16[256,768]{1,0:T(8,128)(2,1)}) custom-call(bf16[256,384]{1,0:T(8,128)(2,1)} %get-tuple-element.9.refs_0_, f32[3,96,384]{2,1,0:T(8,128)} %get-tuple-element.10.refs_1_, bf16[256,768]{1,0:T(8,128)(2,1)} %get-tuple-element.11.refs_2_), custom_call_target="tpu_custom_call" | custom-call | tf_op jit(solution)/shard_map/copy_out/pallas_call | solution.py:811

commit v5 on v4

--- a/solution.py
+++ b/solution.py
@@ -589,6 +589,34 @@
         loop(1, 4, lambda d: copy_w(3 + c, d).start())
         dwr_h[z, c] = dwb_h[z, c]
 
+    for c in rows_sent:
+        c.wait_send()
+
+    def part_of(to):
+        return ht.at[pl.ds(2 * to, 2)]
+
+    def hidden_sum(to, term):
+        pieces = []
+        for i in range(3):
+            rows = pl.ds(pl.multiple_of(to * 768 + i * 256, 256), 256)
+            pieces.append(term(0, rows) + term(1, rows) + term(2, rows))
+        return jnp.concatenate(pieces, axis=0)
+
+    def term_a(c, rows):
+        w = jnp.concatenate([w_v[c, rows, :HD], w_v[c, rows, 2 * HD :]], axis=1)
+        return dot(gx_a[x, c], w, NT)
+
+    def term_shared(c, rows):
+        return dot(gx_h[x, c], w_v[c, rows, HD : 2 * HD], NT)
+
+    def hidden_first(to):
+        part_of(to)[...] = hidden_sum(to, term_a).astype(BF16).reshape(2, NX, 96, T)
+
+    def hidden_part(to):
+        v = part_of(to)[...].astype(F32).reshape(3 * T, T) + hidden_sum(to, term_shared)
+        part_of(to)[...] = v.astype(BF16).reshape(2, NX, 96, T)
+
+    loop(0, 4, hidden_first)
     combine(0, X_ST1)
 
     def send_shared(d):
@@ -607,18 +635,18 @@
     loop(0, 4, prepare_shared)
     ro[2, x] = ob[x]
 
-    forward_a(X_GC, kv_part, mine, 1)
     for kind in (0, 1):
         loop(1, 4, lambda d, kind=kind: copy_k(kind, d).wait_send())
     key_blocks(block_v, 2)
+    forward_a(X_GC, kv_part, mine, 1)
     forward_a(X_GD, kv_part, theirs, 3)
-    key_blocks(block_k, 4)
-
     for d in RING:
         got(C_HX + d, hx.at[xs(4 - d), pl.ds(4 - 4 * core, 4)])
     got_a(X_GA)
     got_a(X_GB)
     weight_a(0)
+    key_blocks(block_k, 4)
+
 
     got_o(2)
     att_ref[:, HD : 2 * HD] = total(ro, 2, 0).astype(BF16)
@@ -652,23 +680,6 @@
     got(Y_K1, y1_r.at[0])
     gx_h[x, 1] = (total(rk, 0, 0) + y1_r[0].astype(F32)).astype(BF16)
     gather_shared(X_GHK, 1)
-
-    for c in rows_sent:
-        c.wait_send()
-
-    def part_of(to):
-        return ht.at[pl.ds(2 * to, 2)]
-
-    def hidden_part(to):
-        pieces = []
-        for i in range(3):
-            v = 0.0
-            for c in range(3):
-                g = jnp.concatenate([gx_a[x, c, :, :HD], gx_h[x, c], gx_a[x, c, :, HD:]], axis=1)
-                rows = pl.ds(pl.multiple_of(to * 768 + i * 256, 256), 256)
-                v = v + dot(g, w_v[c, rows, :], NT)
-            pieces.append(v.astype(BF16))
-        part_of(to)[...] = jnp.concatenate(pieces, axis=0).reshape(2, NX, 96, T)
 
     def copy_mate(i):
         return remote(C_DH + i, part_of(2 * i + 1 - core), dhc.at[i], (me, mate))

time: 103 us -> 102 us (level); the launches traced: 103 us -> 100 us
  Pallas kernels: 102 us -> 99.5 us
    pallas_call x1, Pallas kernels: 100 us -> 97.3 us  [call(): pl.pallas_call(kernel, out_shape=(jax.ShapeDtypeStruct((T, 3 * HD), BF16)...]
where the time goes in v5:
time: 102 us; the launch traced here: 100 us
  Pallas kernels  99.5 us (98%)
    pallas_call x1, Pallas kernels, call(): pl.pallas_call(kernel, out_shape=(jax.ShapeDtypeStruct((T, 3 * HD), BF16)...  97.3 us
    pallas_call x1, Pallas kernels, copy_out(): pl.pallas_call(copy_kernel, out_shape=tuple((jax.ShapeDtypeStruct(a.shape...  2.21 us

profile of v5, /device:TPU:16, one launch (start us, length us, event | category | flops | bytes accessed | tf_op | source)
XLA Modules:
  0.0 100.2 jit_solution(52643244276092381)
XLA Ops:
  0.6 97.3 %attention_with_gradients.1 = (bf16[256,384]{1,0:T(8,128)(2,1)}, f32[3,96,384]{2,1,0:T(8,128)}, bf16[256,768]{1,0:T(8,128)(2,1)}) custom-call(bf16[256,3072]{1,0:T(8,128)(2,1)} %hidden_ref.1, bf16[3,3072,384]{2,1,0:T(8,128)(2,1)} %bitcast.2, bf16[256,384]{1,0:T(8,128)(2,1)} %cot_ref.1), custom_call_target="tpu_custom_call" | custom-call | flops 17999998976 | bytes 10000000 | tf_op jit(solution)/shard_map/attention_with_gradients/pallas_call | solution.py:797
  98.0 2.2 %copy_out.1 = (bf16[256,384]{1,0:T(8,128)(2,1)}, f32[3,96,384]{2,1,0:T(8,128)}, bf16[256,768]{1,0:T(8,128)(2,1)}) custom-call(bf16[256,384]{1,0:T(8,128)(2,1)} %get-tuple-element.9.refs_0_, f32[3,96,384]{2,1,0:T(8,128)} %get-tuple-element.10.refs_1_, bf16[256,768]{1,0:T(8,128)(2,1)} %get-tuple-element.11.refs_2_), custom_call_target="tpu_custom_call" | custom-call | tf_op jit(solution)/shard_map/copy_out/pallas_call | solution.py:822

commit v6 on v5

--- a/solution.py
+++ b/solution.py
@@ -43,7 +43,8 @@
 X_GA, X_GHV, X_GHK, X_GHQ = 47, 51, 55, 67
 C_DH, H_DH = 59, 61
 Y_OA, Y_KA, Y_V1, Y_K1, Y_W1, Y_WA = 62, 63, 64, 65, 66, 83
-X_GB, X_GC, X_GD, N_SEM = 71, 75, 79, 86
+X_GB, X_GC, X_GD, N_SEM = 71, 75, 79, 89
+Y_KVB, Z_KVBR = 11, 85
 RING = (1, 2, 3)
 CROSS_FIRST = (0,)
 
@@ -127,7 +128,8 @@
     for c in local[:3]:
         c.wait()
     project_kv(head_b, far_kv)
-    send(Y_KVA, far_kv, keys_a, partner)
+    send(Y_KVA, far_kv.at[0], keys_a.at[0], partner)
+    send(Y_KVB, far_kv.at[1], keys_a.at[1], partner)
     for c in local[3:5]:
         c.wait()
     project_kv(head_a, keys_a)
@@ -145,9 +147,11 @@
     for d in (1, 3):
         send(X_QGA + d, own_a, own_a, at(z, y, xs(d)))
 
-    got(Y_KVA, kv_rows(1, other, z))
-    for d in (1, 3):
-        send(Z_KVAR + d, kv_rows(1, other, z), kv_rows(1, other, z), at(zs(d), y, x))
+    for part, cross, base in ((0, Y_KVA, Z_KVAR), (1, Y_KVB, Z_KVBR)):
+        piece = kv_rows(1, other, z).at[part]
+        got(cross, piece)
+        for d in (1, 3):
+            send(base + d, piece, piece, at(zs(d), y, x))
 
     def forward_keys(base, yy):
         for part, step in ((0, 1), (1, 3)):
@@ -202,7 +206,12 @@
 
         lax.fori_loop(3, 7, lambda d, _: step(d % 4, _), 0)
 
-    forward_keys(Z_KVAR, other)
+    for part, step, base in ((0, 1, Z_KVAR), (1, 3, Z_KVBR)):
+        piece = kv_rows(1, other, zs(4 - step)).at[part]
+        got(base + step, piece)
+        send(Z_KVAR + 2 - 2 * part, piece, piece, at(zs(step), y, x))
+    got(Z_KVAR + 3, kv_rows(1, other, zs(1)).at[0])
+    got(Z_KVBR + 1, kv_rows(1, other, zs(3)).at[1])
     forward_queries(X_QGR, other)
     transpose_keys(1, Z_KVA, Z_KVAR)
 

time: 102 us -> 101 us (level)
  no operation moved by 1% of the time
where the time goes in v6:
time: 101 us; the launch traced here: 99.5 us
  Pallas kernels  98.8 us (98%)
    pallas_call x1, Pallas kernels, call(): pl.pallas_call(kernel, out_shape=(jax.ShapeDtypeStruct((T, 3 * HD), BF16)...  96.6 us
    pallas_call x1, Pallas kernels, copy_out(): pl.pallas_call(copy_kernel, out_shape=tuple((jax.ShapeDtypeStruct(a.shape...  2.21 us

profile of v6, /device:TPU:16, one launch (start us, length us, event | category | flops | bytes accessed | tf_op | source)
XLA Modules:
  0.0 99.5 jit_solution(859466167951631812)
XLA Ops:
  0.6 96.6 %attention_with_gradients.1 = (bf16[256,384]{1,0:T(8,128)(2,1)}, f32[3,96,384]{2,1,0:T(8,128)}, bf16[256,768]{1,0:T(8,128)(2,1)}) custom-call(bf16[256,3072]{1,0:T(8,128)(2,1)} %hidden_ref.1, bf16[3,3072,384]{2,1,0:T(8,128)(2,1)} %bitcast.2, bf16[256,384]{1,0:T(8,128)(2,1)} %cot_ref.1), custom_call_target="tpu_custom_call" | custom-call | flops 17999998976 | bytes 10000000 | tf_op jit(solution)/shard_map/attention_with_gradients/pallas_call | solution.py:806
  97.3 2.2 %copy_out.1 = (bf16[256,384]{1,0:T(8,128)(2,1)}, f32[3,96,384]{2,1,0:T(8,128)}, bf16[256,768]{1,0:T(8,128)(2,1)}) custom-call(bf16[256,384]{1,0:T(8,128)(2,1)} %get-tuple-element.9.refs_0_, f32[3,96,384]{2,1,0:T(8,128)} %get-tuple-element.10.refs_1_, bf16[256,768]{1,0:T(8,128)(2,1)} %get-tuple-element.11.refs_2_), custom_call_target="tpu_custom_call" | custom-call | tf_op jit(solution)/shard_map/copy_out/pallas_call | solution.py:831
